TPU v7x, 256 devices: a whole 4x4x8 slice. The times are simulated.
256 devices in a mesh: group: 16 (over y_lo, x, core), peer: 16 (over y_hi, z).
Axes of the slice: x: 4, y: 4 (y_hi: 2, y_lo: 2; y = y_hi * 2 + y_lo), z: 8, core: 2. Of those that a mesh axis runs over, the one named last changes fastest.
Arguments:
- dense_feat: bfloat16 [98304, 128], P(('group', 'peer')), may hold values from -6 to 6
- upstream: bfloat16 [98304, 3456], P(('group', 'peer')), may hold values from -0.078125 to 0.078125
- cur_ids: int32 [98304, 26], P(('group', 'peer')), may hold values from 0 to 2047
- work_rows: float32 [524288, 128], P(('group', 'peer')), may hold values from -6 to 6
- work_acc: float32 [524288], P(('group', 'peer')), may hold values from 1.0172526e-05 to 0.00010172526
- cache_table: float32 [131072, 128], P(('group', 'peer')), may hold values from -6 to 6
- home_table: float32 [262144, 128], P(('group', 'peer')), may hold values from -6 to 6
- hit_send: int32 [4096, 64], P(('group', 'peer')), may hold values from 0 to 511
- hit_count: int32 [4096], P(('group', 'peer')), may hold values from 8 to 64, as said below
- miss_send: int32 [4096, 64], P(('group', 'peer')), may hold values from 0 to 1023
- miss_count: int32 [4096], P(('group', 'peer')), may hold values from 8 to 64, as said below
- evict_slot: int32 [4096, 32], P(('group', 'peer')), may hold values from 0 to 2047
- evict_dest: int32 [4096, 32], P(('group', 'peer')), may hold values from 0 to 1023
- evict_count: int32 [4096], P(('group', 'peer')), may hold values from 4 to 32, as said below
- up_proj: bfloat16 [3456, 256], replicated, may hold values from -0.109375 to 0.109375
- down_proj: bfloat16 [256, 3456], replicated, may hold values from -0.375 to 0.375
- cross_bias: float32 [3456], replicated, may hold values from -3 to 3
Outputs:
- next_work: float32 [524288, 128], P(('group', 'peer'))
- work_new: float32 [524288, 128], P(('group', 'peer'))
- home_new: float32 [262144, 128], P(('group', 'peer'))
- grad_up: float32 [3456, 256], P('peer')
- grad_down: float32 [256, 3456], P('peer')
- grad_bias: float32 [3456], P('peer')
Inputs may be any that keep to these rules, and one draw needn't show every extreme that they name: `hit_count`: in every group some peer receives the full 64 rows from every holder of the group. `miss_count`: for every peer index some group receives the full 64 rows from that peer index of every group. `evict_count`: for every peer index some home group receives the full 32 rows from that peer index of every group.
All inputs are finite; a program needn't handle non-finite values.
Results may differ from a plain program's by a relative error of at most 0.007.
Values sent between devices are 32-bit elements; how exact they have to be, the bound alone decides.
A program may use at most 128 MiB of HBM per device.

v0:
```python
import jax
import jax.numpy as jnp
from jax import lax
from jax.sharding import PartitionSpec as P

step_size = 0.5


def contract_rows(left, right):
    return lax.dot_general(
        left, right, (((0,), (0,)), ((), ())), preferred_element_type=jnp.float32
    )


def contract_cols(left, right):
    return lax.dot_general(
        left, right, (((1,), (1,)), ((), ())), preferred_element_type=jnp.float32
    )


def masked_rows(table, listed, counts):
    picked = table[listed.reshape(-1)].reshape(listed.shape[0], listed.shape[1], table.shape[1])
    keep = jnp.arange(listed.shape[1])[None, :] < counts[:, None]
    return jnp.where(keep[:, :, None], picked, jnp.zeros_like(picked))


def body(
    dense_feat,
    upstream,
    cur_ids,
    work_rows,
    work_acc,
    cache_table,
    home_table,
    hit_send,
    hit_count,
    miss_send,
    miss_count,
    evict_slot,
    evict_dest,
    evict_count,
    up_proj,
    down_proj,
    cross_bias,
):
    row_width = work_rows.shape[1]
    batch_rows = cur_ids.shape[0]
    feature_count = cur_ids.shape[1]
    hit_out = masked_rows(cache_table, hit_send, hit_count)
    hit_in = lax.all_to_all(hit_out, "peer", split_axis=0, concat_axis=0, tiled=True)
    miss_out = masked_rows(home_table, miss_send, miss_count)
    miss_in = lax.all_to_all(miss_out, "group", split_axis=0, concat_axis=0, tiled=True)
    flat_ids = cur_ids.reshape(-1)
    looked = work_rows[flat_ids].reshape(batch_rows, feature_count * row_width).astype(jnp.bfloat16)
    stacked = jnp.concatenate([dense_feat, looked], axis=1)
    hidden = jnp.dot(stacked, up_proj, preferred_element_type=jnp.float32).astype(jnp.bfloat16)
    cross_out = jnp.dot(hidden, down_proj, preferred_element_type=jnp.float32) + cross_bias
    gated = (upstream.astype(jnp.float32) * stacked.astype(jnp.float32)).astype(jnp.bfloat16)
    grad_down = contract_rows(hidden, gated)
    grad_bias = jnp.sum(gated.astype(jnp.float32), axis=0)
    back_hidden = contract_cols(gated, down_proj).astype(jnp.bfloat16)
    grad_up = contract_rows(stacked, back_hidden)
    grad_input = upstream.astype(jnp.float32) * (cross_out + 1.0) + contract_cols(
        back_hidden, up_proj
    )
    row_terms = grad_input[:, row_width:].reshape(-1, row_width)
    row_grads = jnp.zeros(work_rows.shape, jnp.float32).at[flat_ids].add(row_terms)
    acc_new = work_acc + jnp.mean(row_grads * row_grads, axis=1)
    row_delta = -step_size * row_grads / jnp.sqrt(acc_new)[:, None]
    work_new = work_rows + row_delta
    evict_out = masked_rows(row_delta, evict_slot, evict_count)
    evict_in = lax.all_to_all(evict_out, "group", split_axis=0, concat_axis=0, tiled=True)
    home_new = home_table.at[evict_dest.reshape(-1)].add(evict_in.reshape(-1, row_width))
    next_work = jnp.concatenate(
        [hit_in.reshape(-1, row_width), miss_in.reshape(-1, row_width)], axis=0
    )
    grad_up, grad_down, grad_bias = lax.psum((grad_up, grad_down, grad_bias), ("group", "peer"))
    position = lax.axis_index("peer")
    pieces = lax.axis_size("peer")
    up_rows = grad_up.shape[0] // pieces
    down_rows = grad_down.shape[0] // pieces
    grad_up = lax.dynamic_slice_in_dim(grad_up, position * up_rows, up_rows, 0)
    grad_down = lax.dynamic_slice_in_dim(grad_down, position * down_rows, down_rows, 0)
    grad_bias = lax.dynamic_slice_in_dim(grad_bias, position * up_rows, up_rows, 0)
    return (next_work, work_new, home_new, grad_up, grad_down, grad_bias)


def solution(mesh):
    return jax.shard_map(
        body,
        mesh=mesh,
        in_specs=(
            P(("group", "peer"), None),
            P(("group", "peer"), None),
            P(("group", "peer"), None),
            P(("group", "peer"), None),
            P(("group", "peer")),
            P(("group", "peer"), None),
            P(("group", "peer"), None),
            P(("group", "peer"), None),
            P(("group", "peer")),
            P(("group", "peer"), None),
            P(("group", "peer")),
            P(("group", "peer"), None),
            P(("group", "peer"), None),
            P(("group", "peer")),
            P(),
            P(),
            P(),
        ),
        out_specs=(
            P(("group", "peer"), None),
            P(("group", "peer"), None),
            P(("group", "peer"), None),
            P("peer", None),
            P("peer", None),
            P("peer"),
        ),
        check_vma=False,
    )
```

profile of v0, /device:TPU:1, one launch (start us, length us, event | category | flops | bytes accessed | tf_op | source)
XLA Modules:
  0.0 339.6 jit_solution(3143062092350771788)
XLA Ops:
  7.2 0.0 copy-start
  7.2 0.0 all-reduce.3.cloned.1.call-start
  7.2 1.2 copy.29
  8.4 0.9 copy.23
  9.4 0.8 reshape.261
  10.2 0.9 fusion.3
  11.1 0.0 copy-start.11
  11.1 0.6 copy-done.11
  11.7 19.2 %gather_fusion.2 = bf16[9984,128]{1,0:T(8,128)(2,1)} fusion(f32[2048,128]{1,0:T(8,128)S(1)} %copy-done.1, s32[10240]{0:T(1024)S(1)} %pad_clamp_fusion), kind=kCustom, calls=%fused_computation.2 | custom fusion | bytes 5151744 | tf_op jit(solution)/shard_map/gather | solution.py:54
  30.9 6.0 %convert_element_type.27 = bf16[384,3328]{1,0:T(8,128)(2,1)} reshape(bf16[9984,128]{1,0:T(8,128)(2,1)} %gather_fusion.2) | data formatting | bytes 5111808 | tf_op jit(solution)/shard_map/convert_element_type | solution.py:54
  37.0 1.9 constant_dynamic-update-slice_fusion
  38.9 0.0 copy-start.5
  38.9 0.0 copy-start.7
  38.9 0.9 convolution_convert_fusion.1
  39.8 1.8 copy-done.5
  41.6 0.5 copy-done.7
  42.1 0.9 convolution_convert_fusion
  43.0 0.0 copy-done.9
  43.1 2.9 fusion.4
  46.0 3.0 fusion.8
  49.0 0.0 all-reduce.3.cloned.1.call-update
  49.0 0.0 copy-start.8
  49.0 0.0 copy-start.10
  49.0 3.2 fusion.7
  52.3 0.0 copy-done.8
  52.3 3.2 fusion.6
  55.5 0.0 copy-done.6
  55.5 2.7 convert_element_type.25
  58.3 0.0 copy-done.15
  58.3 0.1 reshape.264
  58.3 0.1 reshape.258
  58.5 8.6 %slice_add_fusion = f32[384,3328]{1,0:T(8,128)} fusion(f32[384,3456]{1,0:T(8,128)} %fusion.7, f32[384,3456]{1,0:T(8,128)} %convert_element_type.25, f32[384,3456]{1,0:T(8,128)} %fusion.6, f32[3328]{0:T(1024)S(1)} %slice.13), kind=kLoop, calls=%fused_computation.8 | loop fusion | flops 5111808 | bytes 20460544 | tf_op jit(solution)/shard_map/add | solution.py:63
  67.1 6.3 %reshape.303 = f32[9984,128]{1,0:T(8,128)} reshape(f32[384,3328]{1,0:T(8,128)} %slice_add_fusion) | data formatting | bytes 10223616 | tf_op jit(solution)/shard_map/reshape | solution.py:66
  73.4 56.3 %scatter_custom_fusion = f32[2048,128]{1,0:T(8,128)} fusion(s32[9984]{0:T(1024)} %copy-done.11, f32[9984,128]{1,0:T(8,128)} %reshape.303, f32[]{:T(128)} %constant.15.clone.1), kind=kCustom, calls=%fused_computation.17 | custom fusion | flops 1277952 | bytes 1049088 | tf_op jit(solution)/shard_map/scatter-add | solution.py:67
  129.7 1.6 multiply_reduce_fusion
  131.3 0.0 copy-start.19
  131.3 2.9 fusion.5
  134.2 2.3 gather_fusion.3
  136.5 0.1 iota_compare_fusion
  136.6 0.8 broadcast_select_fusion.2
  137.4 7.4 %all-to-all-start.2 = ((f32[16,32,128]{2,1,0:T(8,128)}), f32[16,32,128]{2,1,0:T(8,128)S(1)}, u32[]{:S(2)}, u32[]{:S(2)}) async-start(f32[16,32,128]{2,1,0:T(8,128)} %broadcast_select_fusion.2), calls=%async_computation.2 | async-start | bytes 524288 | tf_op jit(solution)/shard_map/all_to_all | solution.py:72
  144.9 0.1 reshape.255
  145.0 2.8 gather_fusion.1
  147.8 0.1 iota_compare_fusion.1
  147.9 1.0 broadcast_select_fusion
  148.9 3.2 all-to-all-done.2
  152.1 4.2 %all-to-all-start.1 = ((f32[16,64,128]{2,1,0:T(8,128)}), f32[16,64,128]{2,1,0:T(8,128)S(1)}, u32[]{:S(2)}, u32[]{:S(2)}) async-start(f32[16,64,128]{2,1,0:T(8,128)} %broadcast_select_fusion), calls=%async_computation.1 | async-start | bytes 1048576 | tf_op jit(solution)/shard_map/all_to_all | solution.py:52
  156.2 0.0 copy-start.16
  156.3 4.0 %gather_fusion = f32[1024,128]{1,0:T(8,128)} fusion(f32[512,128]{1,0:T(8,128)S(1)} %copy-done.3, s32[1024]{0:T(1024)S(1)} %broadcast_clamp_fusion.1), kind=kCustom, calls=%fused_computation | custom fusion | bytes 1052672 | tf_op jit(solution)/shard_map/gather | solution.py:22
  160.3 0.1 iota_compare_fusion.2
  160.4 2.0 broadcast_select_fusion.1
  162.4 3.8 %all-to-all-done.1 = f32[16,64,128]{2,1,0:T(8,128)S(1)} async-done(((f32[16,64,128]{2,1,0:T(8,128)}), f32[16,64,128]{2,1,0:T(8,128)S(1)}, u32[]{:S(2)}, u32[]{:S(2)}) %all-to-all-start.1) | async-done | bytes 524320 | tf_op jit(solution)/shard_map/all_to_all | solution.py:52
  166.2 10.7 %all-to-all-start = ((f32[16,64,128]{2,1,0:T(8,128)}), f32[16,64,128]{2,1,0:T(8,128)}, u32[]{:S(2)}, u32[]{:S(2)}) async-start(f32[16,64,128]{2,1,0:T(8,128)} %broadcast_select_fusion.1), calls=%async_computation | async-start | bytes 1048576 | tf_op jit(solution)/shard_map/all_to_all | solution.py:50
  176.9 0.1 reshape.263
  177.0 3.3 convert_reduce_fusion
  180.3 76.4 %psum.23 = f32[3456]{0:T(1024)S(1)} all-reduce(f32[3456]{0:T(1024)S(1)} %convert_reduce_fusion), channel_id=1, replica_groups=mesh['group'=16,'peer'=16] {'group','peer'}, use_global_device_ids=true, to_apply=%region_6.7 | all-reduce | flops 3456 | bytes 27648 | tf_op jit(solution)/shard_map/psum | solution.py:77
  256.7 0.6 dynamic_slice.11
  257.3 3.5 %scatter_fusion = f32[1024,128]{1,0:T(8,128)S(1)} fusion(f32[1024,128]{1,0:T(8,128)S(1)} %copy.29, s32[512]{0:T(512)S(1)} %bitcast.27, f32[512,128]{1,0:T(8,128)S(1)} %bitcast.23), kind=kCustom, calls=%fused_computation.5 | custom fusion | flops 65536 | bytes 788480 | tf_op jit(solution)/shard_map/scatter-add | solution.py:73
  260.8 0.0 copy-start.2
  260.8 0.0 all-to-all-done
  260.8 2.3 pad_maximum_fusion
  263.1 66.4 %all-reduce.3.cloned.1.call-done = (f32[3456,256]{1,0:T(8,128)}, f32[256,3456]{1,0:T(8,128)}) async-done(((f32[3456,256]{1,0:T(8,128)}, f32[256,3456]{1,0:T(8,128)}), (f32[3456,256]{1,0:T(8,128)}, f32[256,3456]{1,0:T(8,128)})) %all-reduce.3.cloned.1.call-update) | async-done | bytes 7077904 | tf_op jit(solution)/shard_map/psum | solution.py:77
  329.5 1.6 constant_dynamic-slice_fusion.1
  331.1 1.6 constant_dynamic-slice_fusion
  (38 shorter events, 0.1 us)
Async XLA Ops:
  7.2 31.7 %copy-start = (bf16[3456,256]{1,0:T(8,128)(2,1)S(1)}, bf16[3456,256]{1,0:T(8,128)(2,1)}, u32[]{:S(2)}) copy-start(bf16[3456,256]{1,0:T(8,128)(2,1)} %param.31) | copy-start | bytes 5308420
  7.2 4.5 %copy-start.1 = (f32[2048,128]{1,0:T(8,128)S(1)}, f32[2048,128]{1,0:T(8,128)}, u32[]{:S(2)}) copy-start(f32[2048,128]{1,0:T(8,128)} %param.20) | copy-start | bytes 3145732
  7.2 322.3 %all-reduce.3.cloned.1.call-start = ((), (), s32[]{:S(2)}) async-start(), calls=%async_computation.3 | async-start | bytes 14155776 | tf_op jit(solution)/shard_map/psum | solution.py:77
  11.1 0.6 copy-start.11
  30.9 6.0 %copy-start.12 = (bf16[384,128]{1,0:T(8,128)(2,1)S(1)}, bf16[384,128]{1,0:T(8,128)(2,1)}, u32[]{:S(2)}) copy-start(bf16[384,128]{1,0:T(8,128)(2,1)} %param.17) | copy-start | bytes 294916
  38.9 7.1 %copy-start.4 = (bf16[384,3456]{1,0:T(8,128)(2,1)}, bf16[384,3456]{1,0:T(8,128)(2,1)S(1)}, u32[]{:S(2)}) copy-start(bf16[384,3456]{1,0:T(8,128)(2,1)S(1)} %constant_dynamic-update-slice_fusion) | copy-start | bytes 7962628
  38.9 2.7 copy-start.5
  38.9 3.2 copy-start.7
  42.1 0.9 copy-start.9
  49.0 3.3 copy-start.8
  49.0 3.3 copy-start.10
  52.3 3.2 copy-start.6
  55.5 2.7 copy-start.15
  55.5 2.8 copy-start.17
  55.5 2.9 copy-start.13
  67.1 64.3 %copy-start.14 = (f32[2048]{0:T(1024)S(1)}, f32[2048]{0:T(1024)}, u32[]{:S(2)}) copy-start(f32[2048]{0:T(1024)} %param.21) | copy-start | bytes 24580
  131.3 5.2 %copy-start.19 = (s32[16]{0:T(128)S(1)}, s32[16]{0:T(128)}, u32[]{:S(2)}) copy-start(s32[16]{0:T(128)} %param.30) | copy-start | bytes 196
  134.2 10.7 %copy-start.18 = (s32[16,64]{1,0:T(8,128)S(1)}, s32[16,64]{1,0:T(8,128)}, u32[]{:S(2)}) copy-start(s32[16,64]{1,0:T(8,128)} %param.24) | copy-start | bytes 12292
  137.4 10.3 %copy-start.20 = (s32[16]{0:T(128)S(1)}, s32[16]{0:T(128)}, u32[]{:S(2)}) copy-start(s32[16]{0:T(128)} %param.27) | copy-start | bytes 196
  137.4 14.6 %all-to-all-start.2 = ((f32[16,32,128]{2,1,0:T(8,128)}), f32[16,32,128]{2,1,0:T(8,128)S(1)}, u32[]{:S(2)}, u32[]{:S(2)}) async-start(f32[16,32,128]{2,1,0:T(8,128)} %broadcast_select_fusion.2), calls=%async_computation.2 | async-start | bytes 524288 | tf_op jit(solution)/shard_map/all_to_all | solution.py:72
  145.0 11.3 %copy-start.3 = (f32[512,128]{1,0:T(8,128)S(1)}, f32[512,128]{1,0:T(8,128)}, u32[]{:S(2)}) copy-start(f32[512,128]{1,0:T(8,128)} %param.22) | copy-start | bytes 786436
  148.9 11.4 %copy-start.21 = (s32[16]{0:T(128)S(1)}, s32[16]{0:T(128)}, u32[]{:S(2)}) copy-start(s32[16]{0:T(128)} %param.25) | copy-start | bytes 196
  152.1 14.1 %all-to-all-start.1 = ((f32[16,64,128]{2,1,0:T(8,128)}), f32[16,64,128]{2,1,0:T(8,128)S(1)}, u32[]{:S(2)}, u32[]{:S(2)}) async-start(f32[16,64,128]{2,1,0:T(8,128)} %broadcast_select_fusion), calls=%async_computation.1 | async-start | bytes 1048576 | tf_op jit(solution)/shard_map/all_to_all | solution.py:52
  156.2 20.7 %copy-start.16 = (s32[16,32]{1,0:T(8,128)S(1)}, s32[16,32]{1,0:T(8,128)}, u32[]{:S(2)}) copy-start(s32[16,32]{1,0:T(8,128)} %param.29) | copy-start | bytes 6148
  166.2 94.6 %all-to-all-start = ((f32[16,64,128]{2,1,0:T(8,128)}), f32[16,64,128]{2,1,0:T(8,128)}, u32[]{:S(2)}, u32[]{:S(2)}) async-start(f32[16,64,128]{2,1,0:T(8,128)} %broadcast_select_fusion.1), calls=%async_computation | async-start | bytes 1048576 | tf_op jit(solution)/shard_map/all_to_all | solution.py:50
  260.8 71.9 %copy-start.2 = (f32[1024,128]{1,0:T(8,128)}, f32[1024,128]{1,0:T(8,128)S(1)}, u32[]{:S(2)}) copy-start(f32[1024,128]{1,0:T(8,128)S(1)} %scatter_fusion) | copy-start | bytes 1572868
Sparse Core Ops, SparseCore 0:
  49.1 280.3 all-reduce.2
where the time goes:
time: 341 us; the launch traced here: 340 us
  other arithmetic  86.2 us (25%)
  blocking collectives  76.4 us (22%)
  waiting for transfers between devices  73.4 us (22%)
  local copies, waits for them, and re-layouts  52.8 us (15%)
  starting transfers between devices  22.3 us (7%)
  between operations  14.3 us (4%)
  matrix products  14.2 us (4%)
    psum x1, blocking collectives, body(): lax.psum((grad_up, grad_down, grad_bias), ('group', 'peer'))  76.4 us
    psum x1, waiting for transfers between devices, body(): lax.psum((grad_up, grad_down, grad_bias), ('group', 'peer'))  66.4 us
    scatter-add x1, other arithmetic, body(): jnp.zeros(work_rows.shape, jnp.float32).at[flat_ids].add(row_terms)  56.3 us
    gather x1, local copies, waits for them, and re-layouts, body(): work_rows[flat_ids].reshape(batch_rows, feature_count * row_width)  19.2 us
    all_to_all x1, starting transfers between devices, body(): lax.all_to_all(hit_out, 'peer', split_axis=0, concat_axis=0, tiled=True)  10.7 us
    gather x3, local copies, waits for them, and re-layouts, masked_rows(): table[listed.reshape(-1)]  9.11 us
    add x1, other arithmetic, body(): upstream.astype(jnp.float32) * (cross_out + 1.0)  8.6 us
    all_to_all x1, starting transfers between devices, body(): lax.all_to_all(evict_out, 'group', split_axis=0, concat_axis=0, tiled=True)  7.44 us
  transfers between devices with their start and end apart: 4, of which 3 were waited for; matrix products, arithmetic and copies ran while one was open for 32% of the time, Pallas kernels for 0%

commit v1 on v0

v1 whole, which is shorter than its diff:
```python
import jax
import jax.numpy as jnp
from jax import lax
from jax.experimental import pallas as pl
from jax.experimental.pallas import tpu as pltpu
from jax.sharding import PartitionSpec as P

MESH = pl.DeviceIdType.MESH
F32 = jnp.float32
BF16 = jnp.bfloat16

ROWW = 128
FEAT = 26
RANK = 256
BATCH = 384
WIDTH = 3456
SLOTS = 2048
HOME = 1024
CACHE = 512
HIT = 64
EVICT = 32
FOLD = 4
LINE = SLOTS // FOLD
NG = 16
NP = 16
STEP_SIZE = 0.5


def mm(a, b, dims=((1,), (0,))):
    return lax.dot_general(a, b, (dims, ((), ())), preferred_element_type=F32)


def tile_place(peer, t):
    part, tt = divmod(t, 7)
    return (peer // 8, peer % 8, part // 4, part % 4, tt)


def kernel(
    dense_h, upstream_h, ids_t, rows_h, acc_in, cache_h, home_h, up_h, down_h, bias_in, dest_in,
    hit_send, hit_count, miss_send, miss_count, evict_slot, evict_count,
    next_out, work_out, home_out, gup_out, gdown_out, gbias_out,
    stacked, upstream, gated, up, down, rows, cache, home, idb, folded, hidden, back, hidden_t,
    rg, delta, hit_buf, miss_buf, ev_buf, ev_in,
    grad, r0, ra1, a1, rb1, b1, rc1, c1, ra2, rb2, ab2, rc2, c2, rab, rc3, final, out_all,
    in_sem, hit_s, hit_r, miss_s, miss_r, ev_s, ev_r, core_s, core_r,
    a1_s, a1_r, b1_s, b1_r, c1_s, c1_r, a2_s, a2_r, b2_s, b2_r, c2_s, c2_r,
    z3_s, z3_r, c3_s, c3_r, ag_s, ag_r,
):
    g = lax.axis_index("group")
    p = lax.axis_index("peer")
    core = lax.rem(g, 2)
    x = lax.rem(g // 2, 4)
    yl = g // 8
    yh = p // 8
    z = lax.rem(p, 8)
    y = yh * 2 + yl

    def at_x(c):
        return ((yl * 4 + c) * 2 + core, p)

    def at_y(c):
        return ((lax.rem(c, 2) * 4 + x) * 2 + core, (c // 2) * 8 + z)

    def at_z(c):
        return (g, yh * 8 + c)

    loads = []
    for k, (src, dst) in enumerate((
        (cache_h, cache), (home_h, home), (rows_h, rows), (dense_h, stacked.at[:, 0:ROWW]),
        (upstream_h, upstream), (up_h, up), (down_h, down),
    )):
        c = pltpu.make_async_copy(src, dst, in_sem.at[k])
        c.start()
        loads.append(c)

    barrier = pltpu.get_barrier_semaphore()

    def greet(i, _):
        pl.semaphore_signal(barrier, inc=1, device_id=(lax.rem(g + i, NG), p), device_id_type=MESH)
        pl.semaphore_signal(barrier, inc=1, device_id=(g, lax.rem(p + i, NP)), device_id_type=MESH)
        return 0

    lax.fori_loop(1, 16, greet, 0)
    pl.semaphore_signal(
        barrier, inc=1, device_id=(((1 - yl) * 4 + x) * 2 + core, (1 - yh) * 8 + z), device_id_type=MESH
    )

    def pick(table, listed, counts, buf, many):
        def one(q, _):
            for k in range(many):
                buf[q, pl.ds(k, 1), :] = table[pl.ds(listed[q, k], 1), :]
            keep = lax.broadcasted_iota(jnp.int32, (many, ROWW), 0) < counts[q]
            buf[q] = jnp.where(keep, buf[q], 0.0)
            return 0

        lax.fori_loop(0, 16, one, 0)

    loads[0].wait()
    pick(cache, hit_send, hit_count, hit_buf, HIT)
    loads[1].wait()
    pick(home, miss_send, miss_count, miss_buf, HIT)
    pl.semaphore_wait(barrier, 31)

    def hit_copy(q, to):
        return pltpu.make_async_remote_copy(
            hit_buf.at[to], next_out.at[pl.ds(q * HIT, HIT), :], hit_s.at[to], hit_r.at[q],
            device_id=(g, to), device_id_type=MESH)

    def miss_copy(h, to):
        return pltpu.make_async_remote_copy(
            miss_buf.at[to], next_out.at[pl.ds(NP * HIT + h * HIT, HIT), :], miss_s.at[to], miss_r.at[h],
            device_id=(to, p), device_id_type=MESH)

    def send_rows(i, _):
        hit_copy(p, lax.rem(p + i, NP)).start()
        miss_copy(g, lax.rem(g + i, NG)).start()
        return 0

    lax.fori_loop(1, 16, send_rows, 0)
    next_out[pl.ds(p * HIT, HIT), :] = hit_buf[p]
    next_out[pl.ds(NP * HIT + g * HIT, HIT), :] = miss_buf[g]

    ids_n = jnp.concatenate([ids_t[...], jnp.zeros((ROWW - FEAT, BATCH), jnp.int32)], axis=0).T
    for f in range(FEAT):
        idb[f] = jnp.broadcast_to(ids_n[:, f:f + 1], (BATCH, ROWW))
    loads[2].wait()
    for j in range(FOLD):
        folded[:, j * ROWW:(j + 1) * ROWW] = rows[j * LINE:(j + 1) * LINE, :].astype(BF16)
    loads[3].wait()
    loads[4].wait()
    gated[:, 0:ROWW] = (upstream[:, 0:ROWW].astype(F32) * stacked[:, 0:ROWW].astype(F32)).astype(BF16)

    def look(f, _):
        ids = idb[f]
        low = ids & (LINE - 1)
        lane = lax.broadcasted_iota(jnp.int32, (BATCH, ROWW), 1)
        hot = jnp.concatenate(
            [jnp.where(low == lane + ROWW * j, 1.0, 0.0).astype(BF16) for j in range(LINE // ROWW)], axis=1)
        got = mm(hot, folded[...])
        high = ids >> 9
        row = got[:, 0:ROWW]
        for j in range(1, FOLD):
            row = jnp.where(high == j, got[:, j * ROWW:(j + 1) * ROWW], row)
        cols = pl.ds(pl.multiple_of((f + 1) * ROWW, ROWW), ROWW)
        stacked[:, cols] = row.astype(BF16)
        gated[:, cols] = (upstream[:, cols].astype(F32) * row).astype(BF16)
        return 0

    lax.fori_loop(0, FEAT, look, 0)

    loads[5].wait()
    hidden[...] = mm(stacked[...], up[...]).astype(BF16)
    loads[6].wait()
    back[...] = mm(gated[...], down[...], ((1,), (1,))).astype(BF16)
    hidden_t[0:RANK, :] = hidden[...].astype(F32).T.astype(BF16)
    hidden_t[RANK:, :] = jnp.ones((16, BATCH), BF16)

    sums = []
    for c0 in range(0, 27, 2):
        n = min(2, 27 - c0)
        cols = slice(c0 * ROWW, (c0 + n) * ROWW)
        d = mm(hidden_t[...], gated[:, cols])
        for c in range(n):
            for r in range(32):
                grad[(1,) + tile_place(r // 2, (r % 2) * 27 + c0 + c)] = d[8 * r:8 * r + 8, c * ROWW:(c + 1) * ROWW]
        sums.append(d[RANK:RANK + 8, :])
        u = mm(stacked[:, cols], back[...], ((0,), (0,)))
        for rr in range(16 * n):
            r = c0 * 16 + rr
            for c in range(2):
                grad[(0,) + tile_place(r // 27, (r % 27) * 2 + c)] = u[8 * rr:8 * rr + 8, c * ROWW:(c + 1) * ROWW]
    total = jnp.concatenate(sums + [jnp.zeros((8, 256), F32)], axis=1)
    first = lax.broadcasted_iota(jnp.int32, (8, ROWW), 0) == 0
    nil = jnp.zeros((8, ROWW), F32)
    for q in range(NP):
        start = (216 * q) // ROWW * ROWW
        piece = total[:, start:start + 384]
        if 216 * q > start:
            piece = pltpu.roll(piece, 384 - (216 * q - start), 1)
        grad[(0,) + tile_place(q, 54)] = jnp.where(first, piece[:, 0:ROWW], piece[:, ROWW:2 * ROWW])
        grad[(0,) + tile_place(q, 55)] = nil
        grad[(1,) + tile_place(q, 54)] = nil
        grad[(1,) + tile_place(q, 55)] = nil

    parts = ((6, 7), (0, 3), (3, 6))
    swaps = []
    for k, (lo, hi) in enumerate(parts):
        c = pltpu.make_async_remote_copy(
            grad.at[1 - core, :, :, :, :, lo:hi], r0.at[:, :, :, :, lo:hi], core_s.at[k], core_r.at[k],
            device_id=(g + 1 - 2 * core, p), device_id_type=MESH)
        c.start()
        swaps.append(c)

    def terms(i, _):
        cols = pl.ds(pl.multiple_of(ROWW + i * 256, ROWW), 256)
        cross = mm(hidden[...], down[:, cols])
        bias = bias_in[pl.ds(1 + 2 * i, 2), :]
        bias = jnp.concatenate([bias[0:1], bias[1:2]], axis=1)
        gi = upstream[:, cols].astype(F32) * (cross + bias + 1.0)
        gi = gi + mm(back[...], up[cols, :], ((1,), (1,)))
        for e in range(2):
            f = 2 * i + e
            term = gi[:, e * ROWW:(e + 1) * ROWW]
            high = idb[f] >> 9
            split = jnp.concatenate(
                [jnp.where(high == j, term, 0.0).astype(BF16) for j in range(FOLD)], axis=1)
            low = ids_t[pl.ds(f, 1), :] & (LINE - 1)
            hot = jnp.where(lax.broadcasted_iota(jnp.int32, (LINE, BATCH), 0) == low, 1.0, 0.0).astype(BF16)
            rg[...] += mm(hot, split)
        return 0

    rg[...] = jnp.zeros_like(rg)
    lax.fori_loop(0, 4, terms, 0)

    def ring4(me, dev, chunk, buf, ss, rs):
        right, left = lax.rem(me + 1, 4), lax.rem(me + 3, 4)
        far = lax.rem(me + 2, 4)

        def copy(src, slot, to):
            return pltpu.make_async_remote_copy(
                src, buf.at[slot], ss.at[slot], rs.at[slot], device_id=dev(to), device_id_type=MESH)

        copies = [
            copy(chunk(far, 0), 0, right), copy(chunk(far, 1), 1, left),
            copy(chunk(right, 1), 2, right), copy(chunk(left, 0), 3, left),
            copy(chunk(right, 0), 4, right), copy(chunk(left, 1), 5, left),
        ]

        def start():
            for c in copies[:4]:
                c.start()

        def middle():
            for s, piece in ((0, chunk(right, 0)), (1, chunk(left, 1))):
                copies[s].wait_recv()
                piece[...] = piece[...] + buf[s]
                copies[4 + s].start()

        def finish(put):
            for s in (2, 3, 4, 5):
                copies[s].wait_recv()
            put(0, chunk(me, 0)[...] + buf[3] + buf[4])
            put(1, chunk(me, 1)[...] + buf[2] + buf[5])

        def done():
            for c in copies:
                c.wait_send()

        return start, middle, finish, done

    def direct(n, me, dev, chunk, buf, ss, rs):
        copies = []
        for d in range(1, n):
            to = lax.rem(me + d, n)
            copies.append(pltpu.make_async_remote_copy(
                chunk(to), buf.at[d - 1], ss.at[d - 1], rs.at[d - 1], device_id=dev(to), device_id_type=MESH))

        def start():
            for c in copies:
                c.start()

        def finish():
            for c in copies:
                c.wait_recv()
            s = chunk(me)[...]
            for d in range(n - 1):
                s = s + buf[d]
            return s

        def done():
            for c in copies:
                c.wait_send()

        return start, finish, done

    xa = ring4(x, at_x, lambda c, h: r0.at[h, :, :, c, 0:3], ra1, a1_s, a1_r)
    yb = ring4(y, at_y, lambda c, h: r0.at[c // 2, 4 * h:4 * h + 4, lax.rem(c, 2), :, 3:6], rb1, b1_s, b1_r)
    zc = direct(8, z, at_z, lambda c: r0.at[:, c, :, :, 6], rc1, c1_s, c1_r)
    ya = ring4(y, at_y, lambda c, h: a1.at[c // 2, 4 * h:4 * h + 4, lax.rem(c, 2)], ra2, a2_s, a2_r)
    xb = ring4(x, at_x, lambda c, h: b1.at[4 * h:4 * h + 4, c], rb2, b2_s, b2_r)
    yc = direct(4, y, at_y, lambda c: c1.at[c // 2, lax.rem(c, 2)], rc2, c2_s, c2_r)
    zab = direct(8, z, at_z, lambda c: ab2.at[c], rab, z3_s, z3_r)
    xc = direct(4, x, at_x, lambda c: c2.at[c], rc3, c3_s, c3_r)

    def merge(k, begin):
        lo, hi = parts[k]
        swaps[k].wait_recv()

        def one(q, _):
            a, b = q // 8, lax.rem(q, 8)
            r0[a, b, :, :, lo:hi] = r0[a, b, :, :, lo:hi] + grad[core, a, b, :, :, lo:hi]
            return 0

        lax.fori_loop(0, 16, one, 0)
        begin()

    merge(0, zc[0])
    merge(1, xa[0])
    merge(2, yb[0])

    lax.fori_loop(4, 10, terms, 0)
    xa[1]()
    yb[1]()
    lax.fori_loop(10, 13, terms, 0)

    acc_t = jnp.concatenate([acc_in[...], jnp.zeros((112, ROWW), F32)], axis=0).T
    for b in range(16):
        j, i = divmod(b, 4)
        grads = rg[i * ROWW:(i + 1) * ROWW, j * ROWW:(j + 1) * ROWW]
        new = acc_t[:, b:b + 1] + jnp.mean(grads * grads, axis=1, keepdims=True)
        step = (-STEP_SIZE * grads) / jnp.sqrt(new)
        delta[b * ROWW:(b + 1) * ROWW, :] = step
        work_out[b * ROWW:(b + 1) * ROWW, :] = rows[b * ROWW:(b + 1) * ROWW, :] + step

    pick(delta, evict_slot, evict_count, ev_buf, EVICT)

    def ev_copy(src, to):
        return pltpu.make_async_remote_copy(
            ev_buf.at[to], ev_in.at[src], ev_s.at[to], ev_r.at[src], device_id=(to, p), device_id_type=MESH)

    def send_evicted(i, _):
        ev_copy(g, lax.rem(g + i, NG)).start()
        return 0

    lax.fori_loop(1, 16, send_evicted, 0)
    ev_in[g] = ev_buf[g]

    def put_c1(v):
        c1[...] = v

    put_c1(zc[1]())
    yc[0]()

    def put_a1(h, v):
        a1[h] = v

    xa[2](put_a1)
    ya[0]()

    def put_b1(h, v):
        b1[4 * h:4 * h + 4] = v

    yb[2](put_b1)
    xb[0]()
    c2[...] = yc[1]()
    xc[0]()
    ya[1]()
    xb[1]()

    def put_a2(h, v):
        ab2[4 * h:4 * h + 4, 0:3] = v

    def put_b2(h, v):
        ab2[4 * h:4 * h + 4, 3:6] = v

    ya[2](put_a2)
    xb[2](put_b2)
    zab[0]()

    def got_evicted(i, _):
        ev_copy(lax.rem(g + i, NG), lax.rem(g + i, NG)).wait_recv()
        return 0

    lax.fori_loop(1, 16, got_evicted, 0)
    place = jnp.concatenate([dest_in[k:k + 1, :] for k in range(4)], axis=1)
    hot = jnp.where(lax.broadcasted_iota(jnp.int32, (HOME, NG * EVICT), 0) == place, 1.0, 0.0).astype(BF16)
    home_out[...] = home[...] + mm(hot, ev_in[...].reshape(NG * EVICT, ROWW).astype(BF16))

    final[6] = xc[1]()
    final[0:6] = zab[1]()

    def ag_copy(src, to):
        return pltpu.make_async_remote_copy(
            final, out_all.at[lax.rem(src, 2), src // 8, lax.rem(src // 2, 4)], ag_s.at[to], ag_r.at[src],
            device_id=(to, p), device_id_type=MESH)

    def spread(i, _):
        ag_copy(g, lax.rem(g + i, NG)).start()
        return 0

    lax.fori_loop(1, 16, spread, 0)
    out_all[core, yl, x] = final[...]

    def got_rows(i, _):
        q = lax.rem(p + i, NP)
        h = lax.rem(g + i, NG)
        hit_copy(q, q).wait_recv()
        miss_copy(h, h).wait_recv()
        hit_copy(q, q).wait_send()
        miss_copy(h, h).wait_send()
        ev_copy(h, h).wait_send()
        return 0

    lax.fori_loop(1, 16, got_rows, 0)
    for c in swaps:
        c.wait_send()
    for phase in (xa, yb, zc, ya, xb, yc, zab, xc):
        phase[-1]()

    def got_all(i, _):
        h = lax.rem(g + i, NG)
        ag_copy(h, h).wait()
        return 0

    lax.fori_loop(1, 16, got_all, 0)

    def tile(c, t):
        part, tt = divmod(t, 7)
        return out_all[c, part // 4, part % 4, tt]

    for r in range(27):
        for c in range(2):
            gup_out[8 * r:8 * r + 8, c * ROWW:(c + 1) * ROWW] = tile(0, 2 * r + c)
    for r in range(2):
        for c in range(27):
            gdown_out[8 * r:8 * r + 8, c * ROWW:(c + 1) * ROWW] = tile(1, 27 * r + c)
    gbias_out[...] = tile(0, 54)


def body(
    dense_feat, upstream, cur_ids, work_rows, work_acc, cache_table, home_table, hit_send, hit_count,
    miss_send, miss_count, evict_slot, evict_dest, evict_count, up_proj, down_proj, cross_bias,
):
    vmem = pl.BlockSpec(memory_space=pltpu.VMEM)
    smem = pl.BlockSpec(memory_space=pltpu.SMEM)
    anyw = pl.BlockSpec(memory_space=pl.ANY)
    dma = pltpu.SemaphoreType.DMA
    v = pltpu.VMEM
    t = (8, 128)
    scratch = [
        v((BATCH, WIDTH), BF16), v((BATCH, WIDTH), BF16), v((BATCH, WIDTH), BF16),
        v((WIDTH, RANK), BF16), v((RANK, WIDTH), BF16), v((SLOTS, ROWW), F32), v((CACHE, ROWW), F32),
        v((HOME, ROWW), F32), v((FEAT, BATCH, ROWW), jnp.int32), v((LINE, FOLD * ROWW), BF16),
        v((BATCH, RANK), BF16), v((BATCH, RANK), BF16), v((RANK + 16, BATCH), BF16),
        v((LINE, FOLD * ROWW), F32), v((SLOTS, ROWW), F32),
        v((NP, HIT, ROWW), F32), v((NG, HIT, ROWW), F32), v((NG, EVICT, ROWW), F32), v((NG, EVICT, ROWW), F32),
        v((2, 2, 8, 2, 4, 7) + t, F32), v((2, 8, 2, 4, 7) + t, F32),
        v((6, 8, 2, 3) + t, F32), v((2, 8, 2, 3) + t, F32),
        v((6, 4, 4, 3) + t, F32), v((8, 4, 3) + t, F32),
        v((7, 2, 2, 4) + t, F32), v((2, 2, 4) + t, F32),
        v((6, 4, 3) + t, F32), v((6, 4, 3) + t, F32), v((8, 6) + t, F32),
        v((3, 4) + t, F32), v((4,) + t, F32), v((7, 6) + t, F32), v((3,) + t, F32),
        v((7,) + t, F32), v((2, 2, 4, 7) + t, F32),
        dma((7,)), dma((16,)), dma((16,)), dma((16,)), dma((16,)), dma((16,)), dma((16,)), dma((3,)), dma((3,)),
        dma((6,)), dma((6,)), dma((6,)), dma((6,)), dma((7,)), dma((7,)),
        dma((6,)), dma((6,)), dma((6,)), dma((6,)), dma((3,)), dma((3,)),
        dma((7,)), dma((7,)), dma((3,)), dma((3,)), dma((16,)), dma((16,)),
    ]
    out = pl.pallas_call(
        kernel,
        out_shape=(
            jax.ShapeDtypeStruct((SLOTS, ROWW), F32),
            jax.ShapeDtypeStruct((SLOTS, ROWW), F32),
            jax.ShapeDtypeStruct((HOME, ROWW), F32),
            jax.ShapeDtypeStruct((216, RANK), F32),
            jax.ShapeDtypeStruct((16, WIDTH), F32),
            jax.ShapeDtypeStruct((8, ROWW), F32),
        ),
        in_specs=[anyw, anyw, vmem, anyw, vmem, anyw, anyw, anyw, anyw, vmem, vmem] + [smem] * 6,
        out_specs=(vmem,) * 6,
        scratch_shapes=scratch,
        compiler_params=pltpu.CompilerParams(
            collective_id=0, has_side_effects=True, vmem_limit_bytes=60 * 1024 * 1024),
        name="cross_step",
    )(
        dense_feat, upstream, cur_ids.T, work_rows, work_acc.reshape(16, ROWW), cache_table, home_table,
        up_proj, down_proj, cross_bias.reshape(27, ROWW), evict_dest.reshape(4, ROWW),
        hit_send, hit_count, miss_send, miss_count, evict_slot, evict_count,
    )
    next_work, work_new, home_new, grad_up, grad_down, grad_bias = out
    return next_work, work_new, home_new, grad_up, grad_down, grad_bias.reshape(-1)[:216]


def solution(mesh):
    rows = P(("group", "peer"), None)
    flat = P(("group", "peer"))
    return jax.shard_map(
        body,
        mesh=mesh,
        in_specs=(rows, rows, rows, rows, flat, rows, rows, rows, flat, rows, flat, rows, rows, flat, P(), P(), P()),
        out_specs=(rows, rows, rows, P("peer", None), P("peer", None), P("peer")),
        check_vma=False,
    )
```

time: 341 us -> 84.7 us (0.25)
  other arithmetic: 86.2 us -> 0 us
  blocking collectives: 76.4 us -> 0 us
  Pallas kernels: 0 us -> 75.7 us
  waiting for transfers between devices: 73.4 us -> 0 us
  local copies, waits for them, and re-layouts: 52.8 us -> 8.14 us
  starting transfers between devices: 22.3 us -> 0 us
  matrix products: 14.2 us -> 0 us
  between operations: 14.3 us -> 0.65 us
    psum x1 -> x0, blocking collectives: 76.4 us -> none  [body(): lax.psum((grad_up, grad_down, grad_bias), ('group', 'peer'))]
    pallas_call x0 -> x1, Pallas kernels: none -> 75.7 us  [body(): pl.pallas_call(kernel, out_shape=(jax.ShapeDtypeStruct((SLOTS, ROWW), F32...]
    psum x1 -> x0, waiting for transfers between devices: 66.4 us -> none  [body(): lax.psum((grad_up, grad_down, grad_bias), ('group', 'peer'))]
    scatter-add x2 -> x0, other arithmetic: 59.8 us -> none  [the longest x1 56.3 us: body(): jnp.zeros(work_rows.shape, jnp.float32).at[flat_ids].add(row_terms)]
    gather x4 -> x0, local copies, waits for them, and re-layouts: 28.3 us -> none  [the longest x1 19.2 us: body(): work_rows[flat_ids].reshape(batch_rows, feature_count * row_width)]
    all_to_all x3 -> x0, starting transfers between devices: 22.3 us -> none  [the longest x1 10.7 us: body(): lax.all_to_all(hit_out, 'peer', split_axis=0, concat_axis=0, tiled=True)]
    dot_general x6 -> x0, matrix products: 14.2 us -> none  [the longest x2 5.93 us: contract_rows(): lax.dot_general(left, right, (((0,), (0,)), ((), ())), preferred_element_...]
    add x2 -> x0, other arithmetic: 11.5 us -> none  [the longest x1 8.6 us: body(): upstream.astype(jnp.float32) * (cross_out + 1.0)]
  transfers between devices with their start and end apart: 4 -> 0, of which waited for: 3 -> 0; matrix products, arithmetic and copies ran while one was open for 32% -> 0% of each run, Pallas kernels for 0% -> 0%
where the time goes in v1:
time: 84.7 us; the launch traced here: 84.5 us
  Pallas kernels  75.7 us (89%)
  local copies, waits for them, and re-layouts  8.14 us (10%)
    pallas_call x1, Pallas kernels, body(): pl.pallas_call(kernel, out_shape=(jax.ShapeDtypeStruct((SLOTS, ROWW), F32...  75.7 us
    unnamed x13, local copies, waits for them, and re-layouts  5.47 us

profile of v1, /device:TPU:1, one launch (start us, length us, event | category | flops | bytes accessed | tf_op | source)
XLA Modules:
  0.0 84.5 jit_solution(14218023613372354119)
XLA Ops:
  0.6 1.4 %reshape.26.dest_in = s32[4,128]{1,0:T(4,128)} reshape(s32[16,32]{1,0:T(8,128)} %param.29) | data formatting | bytes 4096 | tf_op jit(solution)/shard_map/reshape | solution.py:467
  2.0 75.7 %cross_step.1 = (f32[2048,128]{1,0:T(8,128)}, f32[2048,128]{1,0:T(8,128)}, f32[1024,128]{1,0:T(8,128)}, f32[216,256]{1,0:T(8,128)}, f32[16,3456]{1,0:T(8,128)}, /*index=5*/f32[8,128]{1,0:T(8,128)}) custom-call(bf16[384,128]{1,0:T(8,128)(2,1)} %dense_h.1, bf16[384,3456]{1,0:T(8,128)(2,1)} %upstream_h.1, s32[26,384]{1,0:T(8,128)} %bitcast.4, ...), custom_call_target="tpu_custom_call" | custom-call | tf_op jit(solution)/shard_map/cross_step/pallas_call | solution.py:449
  77.7 0.0 copy-start
  77.7 1.3 %slice.3 = f32[216]{0:T(256)} slice(f32[1024]{0:T(1024)} %bitcast.7), slice={[0:216]} | slice | bytes 1728 | tf_op jit(solution)/shard_map/slice | solution.py:471
  79.0 0.0 copy-start.1
  79.0 2.3 %copy.28 = f32[2048,128]{1,0:T(8,128)} copy(f32[2048,128]{1,0:T(8,128)} %get-tuple-element.24) | data formatting | bytes 2097152
  81.3 0.0 copy-done
  81.3 0.0 copy-start.3
  81.3 0.0 copy-start.2
  81.3 1.0 %copy.29 = f32[2048,128]{1,0:T(8,128)} copy(f32[2048,128]{1,0:T(8,128)S(1)} %copy-done) | data formatting | bytes 2097152
  82.3 0.0 copy-done.1
  82.3 0.8 copy.30
  83.1 0.0 copy-done.3
  83.1 0.7 copy.31
  83.8 0.0 copy-done.2
  83.8 0.7 copy.32
Async XLA Ops:
  77.7 3.7 %copy-start = (f32[2048,128]{1,0:T(8,128)S(1)}, f32[2048,128]{1,0:T(8,128)}, u32[]{:S(2)}) copy-start(f32[2048,128]{1,0:T(8,128)} %get-tuple-element.25) | copy-start | bytes 3145732
  79.0 3.3 %copy-start.1 = (f32[1024,128]{1,0:T(8,128)S(1)}, f32[1024,128]{1,0:T(8,128)}, u32[]{:S(2)}) copy-start(f32[1024,128]{1,0:T(8,128)} %get-tuple-element.26) | copy-start | bytes 1572868
  81.3 1.8 %copy-start.3 = (f32[216,256]{1,0:T(8,128)S(1)}, f32[216,256]{1,0:T(8,128)}, u32[]{:S(2)}) copy-start(f32[216,256]{1,0:T(8,128)} %get-tuple-element.27) | copy-start | bytes 663556
  81.3 2.5 %copy-start.2 = (f32[16,3456]{1,0:T(8,128)S(1)}, f32[16,3456]{1,0:T(8,128)}, u32[]{:S(2)}) copy-start(f32[16,3456]{1,0:T(8,128)} %get-tuple-element.28) | copy-start | bytes 663556

commit v2 on v1

v2 whole, which is shorter than its diff:
```python
import jax
import jax.numpy as jnp
from jax import lax
from jax.experimental import pallas as pl
from jax.experimental.pallas import tpu as pltpu
from jax.sharding import PartitionSpec as P

MESH = pl.DeviceIdType.MESH
F32 = jnp.float32
BF16 = jnp.bfloat16

ROWW = 128
FEAT = 26
RANK = 256
BATCH = 384
WIDTH = 3456
SLOTS = 2048
HOME = 1024
CACHE = 512
HIT = 64
EVICT = 32
FOLD = 4
LINE = SLOTS // FOLD
NG = 16
NP = 16
STEP_SIZE = 0.5


def mm(a, b, dims=((1,), (0,))):
    return lax.dot_general(a, b, (dims, ((), ())), preferred_element_type=F32)


def tile_place(peer, t):
    part, tt = divmod(t, 7)
    return (peer // 8, peer % 8, part // 4, part % 4, tt)


WAVES = (((0, 2), (2, 4)), ((5, 6), (6, 7)))
Z_TILE = 4
FIRST = 5
T = (8, 128)


def scratch_list():
    v = pltpu.VMEM
    dma = pltpu.SemaphoreType.DMA
    items = [
        ("stacked", v((BATCH, WIDTH), BF16)), ("upstream", v((BATCH, WIDTH), BF16)), ("gated", v((BATCH, WIDTH), BF16)),
        ("up", v((WIDTH, RANK), BF16)), ("down", v((RANK, WIDTH), BF16)), ("rows", v((SLOTS, ROWW), F32)),
        ("cache", v((CACHE, ROWW), F32)), ("home", v((HOME, ROWW), F32)), ("ids_n", v((BATCH, ROWW), jnp.int32)),
        ("idb", v((FEAT, BATCH, ROWW), jnp.int32)), ("folded", v((LINE, FOLD * ROWW), BF16)),
        ("hidden", v((BATCH, RANK), BF16)), ("back", v((BATCH, RANK), BF16)), ("hidden_t", v((RANK + 16, BATCH), BF16)),
        ("rg", v((LINE, FOLD * ROWW), F32)), ("delta", v((SLOTS, ROWW), F32)),
        ("hit_buf", v((NP, HIT, ROWW), F32)), ("miss_buf", v((NG, HIT, ROWW), F32)),
        ("ev_buf", v((NG, EVICT, ROWW), F32)), ("ev_in", v((NG, EVICT, ROWW), F32)),
        ("grad", v((2, 2, 8, 2, 4, 7) + T, F32)), ("r0", v((2, 8, 2, 4, 7) + T, F32)),
        ("rc1", v((7, 2, 2, 4) + T, F32)), ("c1", v((2, 2, 4) + T, F32)), ("rc2", v((3, 4) + T, F32)),
        ("c2", v((4,) + T, F32)), ("rc3", v((3,) + T, F32)),
        ("final", v((7,) + T, F32)), ("out_all", v((2, 2, 4, 7) + T, F32)),
        ("ag_like", v((NG - 1, 7) + T, F32)), ("in_sem", dma((7,))), ("out_sem", dma((2,))), ("core_s", dma((1,))), ("core_r", dma((5,))),
    ]
    for name in ("hit", "miss", "ev", "ag0", "ag1"):
        items += [(name + "_s", dma((1,))), (name + "_r", dma((1,)))]
    for name in ("c1", "c2", "c3"):
        items += [(name + "_s", dma((1,))), (name + "_r", dma((1,)))]
    for w, ((lo, hi), _) in enumerate(WAVES):
        n = hi - lo
        k = str(w)
        items += [
            ("ra1" + k, v((6, 8, 2, n) + T, F32)), ("a1" + k, v((2, 8, 2, n) + T, F32)),
            ("rb1" + k, v((6, 4, 4, n) + T, F32)), ("b1" + k, v((8, 4, n) + T, F32)),
            ("ra2" + k, v((6, 4, n) + T, F32)), ("rb2" + k, v((6, 4, n) + T, F32)),
            ("ab" + k, v((8, 2 * n) + T, F32)), ("rab" + k, v((7, 2 * n) + T, F32)),
        ]
        for name, m in (("xa", 3), ("yb", 3), ("ya", 3), ("xb", 3), ("z", 1)):
            items += [(name + k + "_s", dma((1,))), (name + k + "_r", dma((m,)))]
    return items


class Bag:
    pass


def kernel(*refs):
    names = [
        "dense_h", "upstream_h", "ids_t", "rows_h", "acc_in", "cache_h", "home_h", "up_h", "down_h", "bias_in", "dest_in",
        "hit_send", "hit_count", "miss_send", "miss_count", "evict_slot", "evict_count",
        "next_out", "work_out", "home_out", "gup_out", "gdown_out", "gbias_out",
    ] + [name for name, _ in scratch_list()]
    b = Bag()
    for name, ref in zip(names, refs, strict=True):
        setattr(b, name, ref)
    stacked, upstream, gated, idb, rg = b.stacked, b.upstream, b.gated, b.idb, b.rg

    g = lax.axis_index("group")
    p = lax.axis_index("peer")
    core = lax.rem(g, 2)
    x = lax.rem(g // 2, 4)
    yl = g // 8
    yh = p // 8
    z = lax.rem(p, 8)
    y = yh * 2 + yl

    def at_x(c):
        return ((yl * 4 + c) * 2 + core, p)

    def at_y(c):
        return ((lax.rem(c, 2) * 4 + x) * 2 + core, (c // 2) * 8 + z)

    def at_z(c):
        return (g, yh * 8 + c)

    loads = []
    for k, (src, dst) in enumerate((
        (b.rows_h, b.rows), (b.dense_h, stacked.at[:, 0:ROWW]), (b.upstream_h, upstream),
        (b.cache_h, b.cache), (b.home_h, b.home), (b.up_h, b.up), (b.down_h, b.down),
    )):
        c = pltpu.make_async_copy(src, dst, b.in_sem.at[k])
        c.start()
        loads.append(c)

    barrier = pltpu.get_barrier_semaphore()

    def greet(i, _):
        pl.semaphore_signal(barrier, inc=1, device_id=(lax.rem(g + i, NG), p), device_id_type=MESH)
        pl.semaphore_signal(barrier, inc=1, device_id=(g, lax.rem(p + i, NP)), device_id_type=MESH)
        return 0

    lax.fori_loop(1, 16, greet, 0)
    pl.semaphore_signal(
        barrier, inc=1, device_id=(((1 - yl) * 4 + x) * 2 + core, (1 - yh) * 8 + z), device_id_type=MESH
    )

    def pick(q, table, listed, counts, buf, many):
        for k in range(many):
            buf[q, pl.ds(k, 1), :] = table[pl.ds(listed[q, k], 1), :]
        keep = lax.broadcasted_iota(jnp.int32, (many, ROWW), 0) < counts[q]
        buf[q] = jnp.where(keep, buf[q], 0.0)

    def hit_copy(q, to):
        return pltpu.make_async_remote_copy(
            b.hit_buf.at[to], b.next_out.at[pl.ds(q * HIT, HIT), :], b.hit_s.at[0], b.hit_r.at[0],
            device_id=(g, to), device_id_type=MESH)

    def miss_copy(h, to):
        return pltpu.make_async_remote_copy(
            b.miss_buf.at[to], b.next_out.at[pl.ds(NP * HIT + h * HIT, HIT), :], b.miss_s.at[0], b.miss_r.at[0],
            device_id=(to, p), device_id_type=MESH)

    b.ids_n[...] = jnp.concatenate([b.ids_t[...], jnp.zeros((ROWW - FEAT, BATCH), jnp.int32)], axis=0).T
    loads[0].wait()
    for j in range(FOLD):
        b.folded[:, j * ROWW:(j + 1) * ROWW] = b.rows[j * LINE:(j + 1) * LINE, :].astype(BF16)
    loads[1].wait()
    loads[2].wait()
    gated[:, 0:ROWW] = (upstream[:, 0:ROWW].astype(F32) * stacked[:, 0:ROWW].astype(F32)).astype(BF16)
    loads[3].wait()
    loads[4].wait()

    def look(i):
        turned = pltpu.roll(b.ids_n[...], lax.rem(ROWW - 2 * i, ROWW), 1)
        lane = lax.broadcasted_iota(jnp.int32, (BATCH, ROWW), 1)
        hots = []
        for e in range(2):
            ids = jnp.broadcast_to(turned[:, e:e + 1], (BATCH, ROWW))
            idb[2 * i + e] = ids
            low = ids & (LINE - 1)
            hots.append(jnp.concatenate(
                [jnp.where(low == lane + ROWW * j, 1.0, 0.0).astype(BF16) for j in range(LINE // ROWW)], axis=1))
        got = mm(jnp.concatenate(hots, axis=0), b.folded[...])
        for e in range(2):
            high = idb[2 * i + e] >> 9
            part = got[e * BATCH:(e + 1) * BATCH]
            row = part[:, 0:ROWW]
            for j in range(1, FOLD):
                row = jnp.where(high == j, part[:, j * ROWW:(j + 1) * ROWW], row)
            cols = pl.ds(pl.multiple_of((2 * i + e + 1) * ROWW, ROWW), ROWW)
            stacked[:, cols] = row.astype(BF16)
            gated[:, cols] = (upstream[:, cols].astype(F32) * row).astype(BF16)

    def look_pick(i, _):
        offs = [2 * i + 1, 2 * i + 2]
        for o in offs:
            pick(lax.rem(p + o, NP), b.cache, b.hit_send, b.hit_count, b.hit_buf, HIT)
            pick(lax.rem(g + o, NG), b.home, b.miss_send, b.miss_count, b.miss_buf, HIT)
        look(i)
        for o in offs:
            @pl.when(o < 16)
            def _():
                hit_copy(p, lax.rem(p + o, NP)).start()
                miss_copy(g, lax.rem(g + o, NG)).start()
        return 0

    def look_only(i, _):
        look(i)
        return 0

    pl.semaphore_wait(barrier, 31)
    lax.fori_loop(0, 8, look_pick, 0)
    own_hit = pltpu.make_async_copy(b.hit_buf.at[p], b.next_out.at[pl.ds(p * HIT, HIT), :], b.out_sem.at[0])
    own_miss = pltpu.make_async_copy(
        b.miss_buf.at[g], b.next_out.at[pl.ds(NP * HIT + g * HIT, HIT), :], b.out_sem.at[1])
    own_hit.start()
    own_miss.start()
    lax.fori_loop(8, 13, look_only, 0)

    loads[5].wait()
    b.hidden[...] = mm(stacked[...], b.up[...]).astype(BF16)
    loads[6].wait()
    b.back[...] = mm(gated[...], b.down[...], ((1,), (1,))).astype(BF16)
    b.hidden_t[0:RANK, :] = b.hidden[...].astype(F32).T.astype(BF16)
    b.hidden_t[RANK:, :] = jnp.ones((16, BATCH), BF16)

    sums = []
    grad = b.grad
    for c0 in range(0, 27, 2):
        n = min(2, 27 - c0)
        cols = slice(c0 * ROWW, (c0 + n) * ROWW)
        d = mm(b.hidden_t[...], gated[:, cols])
        for c in range(n):
            for r in range(32):
                grad[(1,) + tile_place(r // 2, (r % 2) * 27 + c0 + c)] = d[8 * r:8 * r + 8, c * ROWW:(c + 1) * ROWW]
        sums.append(d[RANK:RANK + 8, :])
        u = mm(stacked[:, cols], b.back[...], ((0,), (0,)))
        for rr in range(16 * n):
            r = c0 * 16 + rr
            for c in range(2):
                grad[(0,) + tile_place(r // 27, (r % 27) * 2 + c)] = u[8 * rr:8 * rr + 8, c * ROWW:(c + 1) * ROWW]
    total = jnp.concatenate(sums + [jnp.zeros((8, 256), F32)], axis=1)
    first = lax.broadcasted_iota(jnp.int32, (8, ROWW), 0) == 0
    nil = jnp.zeros((8, ROWW), F32)
    for q in range(NP):
        start = (216 * q) // ROWW * ROWW
        piece = total[:, start:start + 384]
        if 216 * q > start:
            piece = pltpu.roll(piece, 384 - (216 * q - start), 1)
        grad[(0,) + tile_place(q, 54)] = jnp.where(first, piece[:, 0:ROWW], piece[:, ROWW:2 * ROWW])
        grad[(0,) + tile_place(q, 55)] = nil
        grad[(1,) + tile_place(q, 54)] = nil
        grad[(1,) + tile_place(q, 55)] = nil

    r0 = b.r0
    parts = ((Z_TILE, Z_TILE + 1),) + WAVES[0] + WAVES[1]
    swaps = []
    for k, (lo, hi) in enumerate(parts):
        c = pltpu.make_async_remote_copy(
            grad.at[1 - core, :, :, :, :, lo:hi], r0.at[:, :, :, :, lo:hi], b.core_s.at[0], b.core_r.at[k],
            device_id=(g + 1 - 2 * core, p), device_id_type=MESH)
        c.start()
        swaps.append(c)

    def merge(k):
        lo, hi = parts[k]
        swaps[k].wait_recv()

        def one(q, _):
            i, j = q // 8, lax.rem(q, 8)
            r0[i, j, :, :, lo:hi] = r0[i, j, :, :, lo:hi] + grad[core, i, j, :, :, lo:hi]
            return 0

        lax.fori_loop(0, 16, one, 0)

    def terms(i, _):
        cols = pl.ds(pl.multiple_of(ROWW + i * 256, ROWW), 256)
        cross = mm(b.hidden[...], b.down[:, cols])
        bias = b.bias_in[pl.ds(1 + 2 * i, 2), :]
        bias = jnp.concatenate([bias[0:1], bias[1:2]], axis=1)
        gi = upstream[:, cols].astype(F32) * (cross + bias + 1.0)
        gi = gi + mm(b.back[...], b.up[cols, :], ((1,), (1,)))
        for e in range(2):
            f = 2 * i + e
            term = gi[:, e * ROWW:(e + 1) * ROWW]
            high = idb[f] >> 9
            split = jnp.concatenate(
                [jnp.where(high == j, term, 0.0).astype(BF16) for j in range(FOLD)], axis=1)
            low = b.ids_t[pl.ds(f, 1), :] & (LINE - 1)
            hot = jnp.where(lax.broadcasted_iota(jnp.int32, (LINE, BATCH), 0) == low, 1.0, 0.0).astype(BF16)
            rg[...] += mm(hot, split)
        return 0

    def await_bytes(ref, sem):
        pltpu.make_async_copy(ref, ref, sem).wait()

    def ring4(me, dev, chunk, buf, ss, rs, put):
        right, left = lax.rem(me + 1, 4), lax.rem(me + 3, 4)
        far = lax.rem(me + 2, 4)

        def copy(src, slot, to):
            return pltpu.make_async_remote_copy(
                src, buf.at[slot], ss.at[0], rs.at[min(slot, 2)], device_id=dev(to), device_id_type=MESH)

        copies = [
            copy(chunk(far, 0), 0, right), copy(chunk(far, 1), 1, left),
            copy(chunk(right, 1), 2, right), copy(chunk(left, 0), 3, left),
            copy(chunk(right, 0), 4, right), copy(chunk(left, 1), 5, left),
        ]

        def start():
            for c in copies[:4]:
                c.start()

        def middle():
            for s, piece in ((0, chunk(right, 0)), (1, chunk(left, 1))):
                copies[s].wait_recv()
                piece[...] = piece[...] + buf[s]
                copies[4 + s].start()

        def finish():
            await_bytes(buf.at[2:6], rs.at[2])
            put(0, chunk(me, 0)[...] + buf[3] + buf[4])
            put(1, chunk(me, 1)[...] + buf[2] + buf[5])

        def done():
            await_bytes(buf, ss.at[0])

        return start, middle, finish, done

    def direct(n, me, dev, chunk, buf, ss, rs, put):
        copies = []
        for d in range(1, n):
            to = lax.rem(me + d, n)
            copies.append(pltpu.make_async_remote_copy(
                chunk(to), buf.at[d - 1], ss.at[0], rs.at[0], device_id=dev(to), device_id_type=MESH))

        def start():
            for c in copies:
                c.start()

        def finish():
            await_bytes(buf, rs.at[0])
            s = chunk(me)[...]
            for d in range(n - 1):
                s = s + buf[d]
            put(s)

        def done():
            await_bytes(buf, ss.at[0])

        return start, finish, done

    def setter(ref, at):
        def put(*v):
            ref[at(*v[:-1])] = v[-1]
        return put

    def sl(lo, hi):
        return slice(lo, hi)

    xa, yb, ya, xb, zw = [], [], [], [], []
    for w, ((alo, ahi), (blo, bhi)) in enumerate(WAVES):
        k = str(w)
        n = ahi - alo
        t = {m: getattr(b, m + k) for m in (
            "ra1", "a1", "rb1", "b1", "ra2", "rb2", "ab", "rab", "xa", "yb", "ya", "xb", "z") if hasattr(b, m + k)}
        sems = {m: (getattr(b, m + k + "_s"), getattr(b, m + k + "_r")) for m in ("xa", "yb", "ya", "xb", "z")}
        xa.append(ring4(
            x, at_x, lambda c, h, lo=alo, hi=ahi: r0.at[h, :, :, c, lo:hi], t["ra1"], *sems["xa"],
            setter(t["a1"], lambda h: h)))
        yb.append(ring4(
            y, at_y, lambda c, h, lo=blo, hi=bhi: r0.at[c // 2, 4 * h:4 * h + 4, lax.rem(c, 2), :, lo:hi],
            t["rb1"], *sems["yb"], setter(t["b1"], lambda h: sl(4 * h, 4 * h + 4))))
        ya.append(ring4(
            y, at_y, lambda c, h, r=t["a1"]: r.at[c // 2, 4 * h:4 * h + 4, lax.rem(c, 2)], t["ra2"], *sems["ya"],
            setter(t["ab"], lambda h, n=n: (sl(4 * h, 4 * h + 4), sl(0, n)))))
        xb.append(ring4(
            x, at_x, lambda c, h, r=t["b1"]: r.at[4 * h:4 * h + 4, c], t["rb2"], *sems["xb"],
            setter(t["ab"], lambda h, n=n: (sl(4 * h, 4 * h + 4), sl(n, 2 * n)))))
        zw.append(direct(
            8, z, at_z, lambda c, r=t["ab"]: r.at[c], t["rab"], *sems["z"],
            setter(b.final, lambda lo=alo, hi=bhi: sl(lo, hi))))
    zc = direct(
        8, z, at_z, lambda c: r0.at[:, c, :, :, Z_TILE], b.rc1, b.c1_s, b.c1_r, setter(b.c1, lambda: Ellipsis))
    yc = direct(
        4, y, at_y, lambda c: b.c1.at[c // 2, lax.rem(c, 2)], b.rc2, b.c2_s, b.c2_r, setter(b.c2, lambda: Ellipsis))
    xc = direct(4, x, at_x, lambda c: b.c2.at[c], b.rc3, b.c3_s, b.c3_r, setter(b.final, lambda: Z_TILE))

    def ev_copy(src, to):
        return pltpu.make_async_remote_copy(
            b.ev_buf.at[to], b.ev_in.at[src], b.ev_s.at[0], b.ev_r.at[0], device_id=(to, p), device_id_type=MESH)

    def adagrad():
        acc_t = jnp.concatenate([b.acc_in[...], jnp.zeros((112, ROWW), F32)], axis=0).T
        for k in range(16):
            j, i = divmod(k, 4)
            grads = rg[i * ROWW:(i + 1) * ROWW, j * ROWW:(j + 1) * ROWW]
            new = acc_t[:, k:k + 1] + jnp.mean(grads * grads, axis=1, keepdims=True)
            step = (-STEP_SIZE * grads) / jnp.sqrt(new)
            b.delta[k * ROWW:(k + 1) * ROWW, :] = step
            b.work_out[k * ROWW:(k + 1) * ROWW, :] = b.rows[k * ROWW:(k + 1) * ROWW, :] + step

    def evict():
        def one(i, _):
            pick(lax.rem(g + i, NG), b.delta, b.evict_slot, b.evict_count, b.ev_buf, EVICT)

            @pl.when(i < 16)
            def _():
                ev_copy(g, lax.rem(g + i, NG)).start()
            return 0

        lax.fori_loop(1, 17, one, 0)
        b.ev_in[g] = b.ev_buf[g]

    def settle_home():
        await_bytes(b.ev_in.at[0:NG - 1], b.ev_r.at[0])
        place = jnp.concatenate([b.dest_in[k:k + 1, :] for k in range(NG)], axis=1)
        hot = jnp.where(lax.broadcasted_iota(jnp.int32, (HOME, NG * EVICT), 0) == place, 1.0, 0.0).astype(BF16)
        b.home_out[...] = b.home[...] + mm(hot, b.ev_in[...].reshape(NG * EVICT, ROWW).astype(BF16))

    def ag_copy(w, src, to):
        lo, hi = ((0, FIRST), (FIRST, 7))[w]
        ss, rs = ((b.ag0_s, b.ag0_r), (b.ag1_s, b.ag1_r))[w]
        return pltpu.make_async_remote_copy(
            b.final.at[lo:hi], b.out_all.at[lax.rem(src, 2), src // 8, lax.rem(src // 2, 4), lo:hi],
            ss.at[0], rs.at[0], device_id=(to, p), device_id_type=MESH)

    def spread(w):
        def one(i, _):
            ag_copy(w, g, lax.rem(g + i, NG)).start()
            return 0

        lax.fori_loop(1, 16, one, 0)
        lo, hi = ((0, FIRST), (FIRST, 7))[w]
        b.out_all[core, yl, x, lo:hi] = b.final[lo:hi]

    def run_terms(lo, hi):
        lax.fori_loop(lo, hi, terms, 0)

    rg[...] = jnp.zeros_like(rg)
    run_terms(0, 1)
    merge(0)
    zc[0]()
    run_terms(1, 2)
    merge(1)
    xa[0][0]()
    merge(2)
    yb[0][0]()
    merge(3)
    merge(4)
    run_terms(2, 6)
    xa[0][1]()
    xa[1][0]()
    yb[0][1]()
    yb[1][0]()
    run_terms(6, 10)
    xa[0][2]()
    ya[0][0]()
    xa[1][1]()
    yb[0][2]()
    xb[0][0]()
    yb[1][1]()
    run_terms(10, 13)
    xa[1][2]()
    ya[1][0]()
    yb[1][2]()
    xb[1][0]()
    ya[0][1]()
    xb[0][1]()
    zc[1]()
    yc[0]()
    adagrad()
    ya[1][1]()
    xb[1][1]()
    ya[0][2]()
    xb[0][2]()
    zw[0][0]()
    evict()
    yc[1]()
    xc[0]()
    ya[1][2]()
    xb[1][2]()
    zw[1][0]()
    xc[1]()
    zw[0][1]()
    spread(0)
    settle_home()
    zw[1][1]()
    spread(1)

    for sems in ((b.hit_s, b.hit_r), (b.miss_s, b.miss_r)):
        for sem in sems:
            await_bytes(b.hit_buf.at[0:NP - 1], sem.at[0])
    await_bytes(b.ev_buf.at[0:NG - 1], b.ev_s.at[0])
    await_bytes(r0, b.core_s.at[0])
    for phase in xa + yb + ya + xb + zw + [zc, yc, xc]:
        phase[-1]()
    own_hit.wait()
    own_miss.wait()
    for (lo, hi), sems in (((0, FIRST), (b.ag0_s, b.ag0_r)), ((FIRST, 7), (b.ag1_s, b.ag1_r))):
        for sem in sems:
            await_bytes(b.ag_like.at[:, lo:hi], sem.at[0])

    def tile(c, t):
        part, tt = divmod(t, 7)
        return b.out_all[c, part // 4, part % 4, tt]

    for r in range(27):
        for c in range(2):
            b.gup_out[8 * r:8 * r + 8, c * ROWW:(c + 1) * ROWW] = tile(0, 2 * r + c)
    for r in range(2):
        for c in range(27):
            b.gdown_out[8 * r:8 * r + 8, c * ROWW:(c + 1) * ROWW] = tile(1, 27 * r + c)
    b.gbias_out[...] = tile(0, 54)


def hand_on(n_in, w_in, h_in, u_in, d_in, b_in, n_out, w_out, h_out, u_out, d_out, b_out, sems):
    copies = []
    for k, (src, dst) in enumerate(zip((n_in, w_in, h_in, u_in, d_in), (n_out, w_out, h_out, u_out, d_out))):
        c = pltpu.make_async_copy(src, dst, sems.at[k])
        c.start()
        copies.append(c)
    b_out[0:ROWW] = b_in[0]
    b_out[ROWW:216] = b_in[1, 0:216 - ROWW]
    for c in copies:
        c.wait()


def body(
    dense_feat, upstream, cur_ids, work_rows, work_acc, cache_table, home_table, hit_send, hit_count,
    miss_send, miss_count, evict_slot, evict_dest, evict_count, up_proj, down_proj, cross_bias,
):
    vmem = pl.BlockSpec(memory_space=pltpu.VMEM)
    smem = pl.BlockSpec(memory_space=pltpu.SMEM)
    anyw = pl.BlockSpec(memory_space=pl.ANY)
    shapes = [
        jax.ShapeDtypeStruct(s, F32)
        for s in ((SLOTS, ROWW), (SLOTS, ROWW), (HOME, ROWW), (216, RANK), (16, WIDTH), (8, ROWW))
    ]
    out = pl.pallas_call(
        kernel,
        out_shape=tuple(pltpu.VMEM(s.shape, F32) for s in shapes),
        in_specs=[anyw, anyw, vmem, anyw, vmem, anyw, anyw, anyw, anyw, vmem, vmem] + [smem] * 6,
        out_specs=(vmem,) * 6,
        scratch_shapes=[s for _, s in scratch_list()],
        compiler_params=pltpu.CompilerParams(
            collective_id=0, has_side_effects=True, vmem_limit_bytes=60 * 1024 * 1024),
        name="cross_step",
    )(
        dense_feat, upstream, cur_ids.T, work_rows, work_acc.reshape(16, ROWW), cache_table, home_table,
        up_proj, down_proj, cross_bias.reshape(27, ROWW), evict_dest,
        hit_send, hit_count, miss_send, miss_count, evict_slot, evict_count,
    )
    return pl.pallas_call(
        hand_on,
        out_shape=tuple(shapes[:5]) + (jax.ShapeDtypeStruct((216,), F32),),
        in_specs=[vmem] * 6,
        out_specs=(anyw,) * 5 + (vmem,),
        scratch_shapes=[pltpu.SemaphoreType.DMA((5,))],
        compiler_params=pltpu.CompilerParams(vmem_limit_bytes=4 * 1024 * 1024),
        name="hand_on",
    )(*[pltpu.with_memory_space_constraint(o, pltpu.VMEM) for o in out])


def solution(mesh):
    rows = P(("group", "peer"), None)
    flat = P(("group", "peer"))
    return jax.shard_map(
        body,
        mesh=mesh,
        in_specs=(rows, rows, rows, rows, flat, rows, rows, rows, flat, rows, flat, rows, rows, flat, P(), P(), P()),
        out_specs=(rows, rows, rows, P("peer", None), P("peer", None), P("peer")),
        check_vma=False,
    )
```

time: 84.7 us -> 72.2 us (0.85)
  local copies, waits for them, and re-layouts: 8.14 us -> 0 us
  Pallas kernels: 75.7 us -> 71.4 us
    unnamed x13 -> x0, local copies, waits for them, and re-layouts: 5.47 us -> none
    pallas_call x1 -> x2, Pallas kernels: 75.7 us -> 71.4 us  [the longest x1 69.2 us: body(): pl.pallas_call(kernel, out_shape=tuple((pltpu.VMEM(s.shape, F32) for s in...]
    reshape x1 -> x0, local copies, waits for them, and re-layouts: 1.35 us -> none  [body(): evict_dest.reshape(4, ROWW)]
    slice x1 -> x0, local copies, waits for them, and re-layouts: 1.32 us -> none  [body(): grad_bias.reshape(-1)[:216]]
where the time goes in v2:
time: 72.2 us; the launch traced here: 72 us
  Pallas kernels  71.4 us (99%)
    pallas_call x1, Pallas kernels, body(): pl.pallas_call(kernel, out_shape=tuple((pltpu.VMEM(s.shape, F32) for s in...  69.2 us
    pallas_call x1, Pallas kernels, body(): pl.pallas_call(hand_on, out_shape=tuple(shapes[:5]) + (jax.ShapeDtypeStru...  2.23 us

profile of v2, /device:TPU:1, one launch (start us, length us, event | category | flops | bytes accessed | tf_op | source)
XLA Modules:
  0.0 72.0 jit_solution(13983734525300118555)
XLA Ops:
  0.6 69.2 %cross_step.1 = (f32[2048,128]{1,0:T(8,128)S(1)}, f32[2048,128]{1,0:T(8,128)S(1)}, f32[1024,128]{1,0:T(8,128)S(1)}, f32[216,256]{1,0:T(8,128)S(1)}, f32[16,3456]{1,0:T(8,128)S(1)}, /*index=5*/f32[8,128]{1,0:T(8,128)S(1)}) custom-call(bf16[384,128]{1,0:T(8,128)(2,1)} %refs_0_.1, bf16[384,3456]{1,0:T(8,128)(2,1)} %refs_1_.1, s32[26,384]{1,0:T(8,128)} %bitcast.3, ...), custom_call_target="tpu_custom_call" | custom-call | tf_op jit(solution)/shard_map/cross_step/pallas_call | solution.py:528
  69.8 2.2 %hand_on.1 = (f32[2048,128]{1,0:T(8,128)}, f32[2048,128]{1,0:T(8,128)}, f32[1024,128]{1,0:T(8,128)}, f32[216,256]{1,0:T(8,128)}, f32[16,3456]{1,0:T(8,128)}, /*index=5*/f32[216]{0:T(256)}) custom-call(f32[2048,128]{1,0:T(8,128)S(1)} %get-tuple-element.12.n_in, f32[2048,128]{1,0:T(8,128)S(1)} %get-tuple-element.13.w_in, ...), custom_call_target="tpu_custom_call" | custom-call | tf_op jit(solution)/shard_map/hand_on/pallas_call | solution.py:542

commit v3 on v2

--- a/solution.py
+++ b/solution.py
@@ -37,7 +37,9 @@
 
 WAVES = (((0, 2), (2, 4)), ((5, 6), (6, 7)))
 Z_TILE = 4
-FIRST = 5
+FIRST = 4
+SPANS = ((0, FIRST), (FIRST, 7))
+LOOKS = ((0, 7), (7, 14), (14, 20), (20, 26))
 T = (8, 128)
 
 
@@ -48,6 +50,8 @@
         ("stacked", v((BATCH, WIDTH), BF16)), ("upstream", v((BATCH, WIDTH), BF16)), ("gated", v((BATCH, WIDTH), BF16)),
         ("up", v((WIDTH, RANK), BF16)), ("down", v((RANK, WIDTH), BF16)), ("rows", v((SLOTS, ROWW), F32)),
         ("cache", v((CACHE, ROWW), F32)), ("home", v((HOME, ROWW), F32)), ("ids_n", v((BATCH, ROWW), jnp.int32)),
+        ("ids_t", v((FEAT, BATCH), jnp.int32)), ("acc_in", v((16, ROWW), F32)), ("bias_in", v((27, ROWW), F32)),
+        ("dest_in", v((NG, EVICT), jnp.int32)),
         ("idb", v((FEAT, BATCH, ROWW), jnp.int32)), ("folded", v((LINE, FOLD * ROWW), BF16)),
         ("hidden", v((BATCH, RANK), BF16)), ("back", v((BATCH, RANK), BF16)), ("hidden_t", v((RANK + 16, BATCH), BF16)),
         ("rg", v((LINE, FOLD * ROWW), F32)), ("delta", v((SLOTS, ROWW), F32)),
@@ -57,7 +61,7 @@
         ("rc1", v((7, 2, 2, 4) + T, F32)), ("c1", v((2, 2, 4) + T, F32)), ("rc2", v((3, 4) + T, F32)),
         ("c2", v((4,) + T, F32)), ("rc3", v((3,) + T, F32)),
         ("final", v((7,) + T, F32)), ("out_all", v((2, 2, 4, 7) + T, F32)),
-        ("ag_like", v((NG - 1, 7) + T, F32)), ("in_sem", dma((7,))), ("out_sem", dma((2,))), ("core_s", dma((1,))), ("core_r", dma((5,))),
+        ("ag_like", v((7, 7) + T, F32)), ("fw_s", dma((2,))), ("fw_r", dma((2,))), ("in_sem", dma((11,))), ("out_sem", dma((2,))), ("core_s", dma((1,))), ("core_r", dma((5,))),
     ]
     for name in ("hit", "miss", "ev", "ag0", "ag1"):
         items += [(name + "_s", dma((1,))), (name + "_r", dma((1,)))]
@@ -69,10 +73,10 @@
         items += [
             ("ra1" + k, v((6, 8, 2, n) + T, F32)), ("a1" + k, v((2, 8, 2, n) + T, F32)),
             ("rb1" + k, v((6, 4, 4, n) + T, F32)), ("b1" + k, v((8, 4, n) + T, F32)),
-            ("ra2" + k, v((6, 4, n) + T, F32)), ("rb2" + k, v((6, 4, n) + T, F32)),
+            ("ra2" + k, v((3, 8, n) + T, F32)), ("rb2" + k, v((3, 8, n) + T, F32)),
             ("ab" + k, v((8, 2 * n) + T, F32)), ("rab" + k, v((7, 2 * n) + T, F32)),
         ]
-        for name, m in (("xa", 3), ("yb", 3), ("ya", 3), ("xb", 3), ("z", 1)):
+        for name, m in (("xa", 3), ("yb", 3), ("ya", 1), ("xb", 1), ("z", 1)):
             items += [(name + k + "_s", dma((1,))), (name + k + "_r", dma((m,)))]
     return items
 
@@ -83,7 +87,7 @@
 
 def kernel(*refs):
     names = [
-        "dense_h", "upstream_h", "ids_t", "rows_h", "acc_in", "cache_h", "home_h", "up_h", "down_h", "bias_in", "dest_in",
+        "dense_h", "upstream_h", "ids_h", "rows_h", "acc_h", "cache_h", "home_h", "up_h", "down_h", "bias_h", "dest_h",
         "hit_send", "hit_count", "miss_send", "miss_count", "evict_slot", "evict_count",
         "next_out", "work_out", "home_out", "gup_out", "gdown_out", "gbias_out",
     ] + [name for name, _ in scratch_list()]
@@ -110,14 +114,15 @@
     def at_z(c):
         return (g, yh * 8 + c)
 
-    loads = []
-    for k, (src, dst) in enumerate((
-        (b.rows_h, b.rows), (b.dense_h, stacked.at[:, 0:ROWW]), (b.upstream_h, upstream),
-        (b.cache_h, b.cache), (b.home_h, b.home), (b.up_h, b.up), (b.down_h, b.down),
+    loads = {}
+    for k, (name, src, dst) in enumerate((
+        ("ids", b.ids_h, b.ids_t), ("cache", b.cache_h, b.cache), ("home", b.home_h, b.home), ("rows", b.rows_h, b.rows),
+        ("dense", b.dense_h, stacked.at[:, 0:ROWW]), ("upstream", b.upstream_h, upstream),
+        ("up", b.up_h, b.up), ("down", b.down_h, b.down),
+        ("acc", b.acc_h, b.acc_in), ("bias", b.bias_h, b.bias_in), ("dest", b.dest_h, b.dest_in),
     )):
-        c = pltpu.make_async_copy(src, dst, b.in_sem.at[k])
-        c.start()
-        loads.append(c)
+        loads[name] = pltpu.make_async_copy(src, dst, b.in_sem.at[k])
+        loads[name].start()
 
     barrier = pltpu.get_barrier_semaphore()
 
@@ -147,107 +152,120 @@
             b.miss_buf.at[to], b.next_out.at[pl.ds(NP * HIT + h * HIT, HIT), :], b.miss_s.at[0], b.miss_r.at[0],
             device_id=(to, p), device_id_type=MESH)
 
+    def pick_out(o):
+        pick(lax.rem(p + o, NP), b.cache, b.hit_send, b.hit_count, b.hit_buf, HIT)
+        pick(lax.rem(g + o, NG), b.home, b.miss_send, b.miss_count, b.miss_buf, HIT)
+        return 0
+
+    loads["ids"].wait()
     b.ids_n[...] = jnp.concatenate([b.ids_t[...], jnp.zeros((ROWW - FEAT, BATCH), jnp.int32)], axis=0).T
-    loads[0].wait()
+    loads["cache"].wait()
+    loads["home"].wait()
+    lax.fori_loop(1, 17, lambda o, _: pick_out(o), 0)
+    loads["rows"].wait()
     for j in range(FOLD):
         b.folded[:, j * ROWW:(j + 1) * ROWW] = b.rows[j * LINE:(j + 1) * LINE, :].astype(BF16)
-    loads[1].wait()
-    loads[2].wait()
+    loads["dense"].wait()
+    loads["upstream"].wait()
     gated[:, 0:ROWW] = (upstream[:, 0:ROWW].astype(F32) * stacked[:, 0:ROWW].astype(F32)).astype(BF16)
-    loads[3].wait()
-    loads[4].wait()
-
-    def look(i):
-        turned = pltpu.roll(b.ids_n[...], lax.rem(ROWW - 2 * i, ROWW), 1)
+
+    def look(lo, hi):
         lane = lax.broadcasted_iota(jnp.int32, (BATCH, ROWW), 1)
         hots = []
-        for e in range(2):
-            ids = jnp.broadcast_to(turned[:, e:e + 1], (BATCH, ROWW))
-            idb[2 * i + e] = ids
+        for f in range(lo, hi):
+            ids = jnp.broadcast_to(b.ids_n[:, f:f + 1], (BATCH, ROWW))
+            idb[f] = ids
             low = ids & (LINE - 1)
             hots.append(jnp.concatenate(
                 [jnp.where(low == lane + ROWW * j, 1.0, 0.0).astype(BF16) for j in range(LINE // ROWW)], axis=1))
         got = mm(jnp.concatenate(hots, axis=0), b.folded[...])
-        for e in range(2):
-            high = idb[2 * i + e] >> 9
+        for e, f in enumerate(range(lo, hi)):
+            high = idb[f] >> 9
             part = got[e * BATCH:(e + 1) * BATCH]
             row = part[:, 0:ROWW]
             for j in range(1, FOLD):
                 row = jnp.where(high == j, part[:, j * ROWW:(j + 1) * ROWW], row)
-            cols = pl.ds(pl.multiple_of((2 * i + e + 1) * ROWW, ROWW), ROWW)
+            cols = slice((f + 1) * ROWW, (f + 2) * ROWW)
             stacked[:, cols] = row.astype(BF16)
             gated[:, cols] = (upstream[:, cols].astype(F32) * row).astype(BF16)
 
-    def look_pick(i, _):
-        offs = [2 * i + 1, 2 * i + 2]
-        for o in offs:
-            pick(lax.rem(p + o, NP), b.cache, b.hit_send, b.hit_count, b.hit_buf, HIT)
-            pick(lax.rem(g + o, NG), b.home, b.miss_send, b.miss_count, b.miss_buf, HIT)
-        look(i)
-        for o in offs:
-            @pl.when(o < 16)
-            def _():
-                hit_copy(p, lax.rem(p + o, NP)).start()
-                miss_copy(g, lax.rem(g + o, NG)).start()
+    pl.semaphore_wait(barrier, 31)
+
+    def send_rows(o, _):
+        hit_copy(p, lax.rem(p + o, NP)).start()
+        miss_copy(g, lax.rem(g + o, NG)).start()
         return 0
 
-    def look_only(i, _):
-        look(i)
-        return 0
-
-    pl.semaphore_wait(barrier, 31)
-    lax.fori_loop(0, 8, look_pick, 0)
+    lax.fori_loop(1, 16, send_rows, 0)
     own_hit = pltpu.make_async_copy(b.hit_buf.at[p], b.next_out.at[pl.ds(p * HIT, HIT), :], b.out_sem.at[0])
     own_miss = pltpu.make_async_copy(
         b.miss_buf.at[g], b.next_out.at[pl.ds(NP * HIT + g * HIT, HIT), :], b.out_sem.at[1])
     own_hit.start()
     own_miss.start()
-    lax.fori_loop(8, 13, look_only, 0)
-
-    loads[5].wait()
-    b.hidden[...] = mm(stacked[...], b.up[...]).astype(BF16)
-    loads[6].wait()
-    b.back[...] = mm(gated[...], b.down[...], ((1,), (1,))).astype(BF16)
-    b.hidden_t[0:RANK, :] = b.hidden[...].astype(F32).T.astype(BF16)
-    b.hidden_t[RANK:, :] = jnp.ones((16, BATCH), BF16)
-
-    sums = []
-    grad = b.grad
-    for c0 in range(0, 27, 2):
-        n = min(2, 27 - c0)
-        cols = slice(c0 * ROWW, (c0 + n) * ROWW)
-        d = mm(b.hidden_t[...], gated[:, cols])
-        for c in range(n):
-            for r in range(32):
-                grad[(1,) + tile_place(r // 2, (r % 2) * 27 + c0 + c)] = d[8 * r:8 * r + 8, c * ROWW:(c + 1) * ROWW]
-        sums.append(d[RANK:RANK + 8, :])
-        u = mm(stacked[:, cols], b.back[...], ((0,), (0,)))
-        for rr in range(16 * n):
-            r = c0 * 16 + rr
-            for c in range(2):
-                grad[(0,) + tile_place(r // 27, (r % 27) * 2 + c)] = u[8 * rr:8 * rr + 8, c * ROWW:(c + 1) * ROWW]
-    total = jnp.concatenate(sums + [jnp.zeros((8, 256), F32)], axis=1)
-    first = lax.broadcasted_iota(jnp.int32, (8, ROWW), 0) == 0
-    nil = jnp.zeros((8, ROWW), F32)
-    for q in range(NP):
-        start = (216 * q) // ROWW * ROWW
-        piece = total[:, start:start + 384]
-        if 216 * q > start:
-            piece = pltpu.roll(piece, 384 - (216 * q - start), 1)
-        grad[(0,) + tile_place(q, 54)] = jnp.where(first, piece[:, 0:ROWW], piece[:, ROWW:2 * ROWW])
-        grad[(0,) + tile_place(q, 55)] = nil
-        grad[(1,) + tile_place(q, 54)] = nil
-        grad[(1,) + tile_place(q, 55)] = nil
-
-    r0 = b.r0
-    parts = ((Z_TILE, Z_TILE + 1),) + WAVES[0] + WAVES[1]
+    for lo, hi in LOOKS:
+        look(lo, hi)
+
+    grad, r0 = b.grad, b.r0
+    parts = WAVES[0] + ((Z_TILE, Z_TILE + 1),) + WAVES[1]
     swaps = []
     for k, (lo, hi) in enumerate(parts):
-        c = pltpu.make_async_remote_copy(
+        swaps.append(pltpu.make_async_remote_copy(
             grad.at[1 - core, :, :, :, :, lo:hi], r0.at[:, :, :, :, lo:hi], b.core_s.at[0], b.core_r.at[k],
-            device_id=(g + 1 - 2 * core, p), device_id_type=MESH)
-        c.start()
-        swaps.append(c)
+            device_id=(g + 1 - 2 * core, p), device_id_type=MESH))
+
+    loads["up"].wait()
+    loads["down"].wait()
+    blocks = [(c0, min(2, 27 - c0)) for c0 in range(0, 27, 2)]
+    nil = jnp.zeros((8, ROWW), F32)
+
+    def down_grad():
+        b.hidden[...] = mm(stacked[...], b.up[...]).astype(BF16)
+        b.hidden_t[0:RANK, :] = b.hidden[...].astype(F32).T.astype(BF16)
+        b.hidden_t[RANK:, :] = jnp.ones((16, BATCH), BF16)
+        sums = []
+        for c0, n in blocks:
+            d = mm(b.hidden_t[...], gated[:, c0 * ROWW:(c0 + n) * ROWW])
+            for c in range(n):
+                for r in range(32):
+                    grad[(1,) + tile_place(r // 2, (r % 2) * 27 + c0 + c)] = (
+                        d[8 * r:8 * r + 8, c * ROWW:(c + 1) * ROWW])
+            sums.append(d[RANK:RANK + 8, :])
+        total = jnp.concatenate(sums + [jnp.zeros((8, 256), F32)], axis=1)
+        first = lax.broadcasted_iota(jnp.int32, (8, ROWW), 0) == 0
+        for q in range(NP):
+            start = (216 * q) // ROWW * ROWW
+            piece = total[:, start:start + 384]
+            if 216 * q > start:
+                piece = pltpu.roll(piece, 384 - (216 * q - start), 1)
+            grad[(1,) + tile_place(q, 54)] = jnp.where(first, piece[:, 0:ROWW], piece[:, ROWW:2 * ROWW])
+            grad[(1,) + tile_place(q, 55)] = nil
+
+    def up_grad():
+        b.back[...] = mm(gated[...], b.down[...], ((1,), (1,))).astype(BF16)
+        for c0, n in blocks:
+            u = mm(stacked[:, c0 * ROWW:(c0 + n) * ROWW], b.back[...], ((0,), (0,)))
+            for rr in range(16 * n):
+                r = c0 * 16 + rr
+                for c in range(2):
+                    grad[(0,) + tile_place(r // 27, (r % 27) * 2 + c)] = (
+                        u[8 * rr:8 * rr + 8, c * ROWW:(c + 1) * ROWW])
+        for q in range(NP):
+            grad[(0,) + tile_place(q, 54)] = nil
+            grad[(0,) + tile_place(q, 55)] = nil
+
+    @pl.when(core == 0)
+    def _():
+        down_grad()
+        for c in swaps:
+            c.start()
+        up_grad()
+
+    @pl.when(core == 1)
+    def _():
+        up_grad()
+        for c in swaps:
+            c.start()
+        down_grad()
 
     def merge(k):
         lo, hi = parts[k]
@@ -267,15 +285,17 @@
         bias = jnp.concatenate([bias[0:1], bias[1:2]], axis=1)
         gi = upstream[:, cols].astype(F32) * (cross + bias + 1.0)
         gi = gi + mm(b.back[...], b.up[cols, :], ((1,), (1,)))
+        hots, splits = [], []
         for e in range(2):
             f = 2 * i + e
             term = gi[:, e * ROWW:(e + 1) * ROWW]
             high = idb[f] >> 9
-            split = jnp.concatenate(
-                [jnp.where(high == j, term, 0.0).astype(BF16) for j in range(FOLD)], axis=1)
+            splits.append(jnp.concatenate(
+                [jnp.where(high == j, term, 0.0).astype(BF16) for j in range(FOLD)], axis=1))
             low = b.ids_t[pl.ds(f, 1), :] & (LINE - 1)
-            hot = jnp.where(lax.broadcasted_iota(jnp.int32, (LINE, BATCH), 0) == low, 1.0, 0.0).astype(BF16)
-            rg[...] += mm(hot, split)
+            hots.append(jnp.where(
+                lax.broadcasted_iota(jnp.int32, (LINE, BATCH), 0) == low, 1.0, 0.0).astype(BF16))
+        rg[...] += mm(jnp.concatenate(hots, axis=1), jnp.concatenate(splits, axis=0))
         return 0
 
     def await_bytes(ref, sem):
@@ -359,12 +379,12 @@
         yb.append(ring4(
             y, at_y, lambda c, h, lo=blo, hi=bhi: r0.at[c // 2, 4 * h:4 * h + 4, lax.rem(c, 2), :, lo:hi],
             t["rb1"], *sems["yb"], setter(t["b1"], lambda h: sl(4 * h, 4 * h + 4))))
-        ya.append(ring4(
-            y, at_y, lambda c, h, r=t["a1"]: r.at[c // 2, 4 * h:4 * h + 4, lax.rem(c, 2)], t["ra2"], *sems["ya"],
-            setter(t["ab"], lambda h, n=n: (sl(4 * h, 4 * h + 4), sl(0, n)))))
-        xb.append(ring4(
-            x, at_x, lambda c, h, r=t["b1"]: r.at[4 * h:4 * h + 4, c], t["rb2"], *sems["xb"],
-            setter(t["ab"], lambda h, n=n: (sl(4 * h, 4 * h + 4), sl(n, 2 * n)))))
+        ya.append(direct(
+            4, y, at_y, lambda c, r=t["a1"]: r.at[c // 2, :, lax.rem(c, 2)], t["ra2"], *sems["ya"],
+            setter(t["ab"], lambda n=n: (slice(None), sl(0, n)))))
+        xb.append(direct(
+            4, x, at_x, lambda c, r=t["b1"]: r.at[:, c], t["rb2"], *sems["xb"],
+            setter(t["ab"], lambda n=n: (slice(None), sl(n, 2 * n)))))
         zw.append(direct(
             8, z, at_z, lambda c, r=t["ab"]: r.at[c], t["rab"], *sems["z"],
             setter(b.final, lambda lo=alo, hi=bhi: sl(lo, hi))))
@@ -384,7 +404,7 @@
             j, i = divmod(k, 4)
             grads = rg[i * ROWW:(i + 1) * ROWW, j * ROWW:(j + 1) * ROWW]
             new = acc_t[:, k:k + 1] + jnp.mean(grads * grads, axis=1, keepdims=True)
-            step = (-STEP_SIZE * grads) / jnp.sqrt(new)
+            step = grads * (-STEP_SIZE * lax.rsqrt(new))
             b.delta[k * ROWW:(k + 1) * ROWW, :] = step
             b.work_out[k * ROWW:(k + 1) * ROWW, :] = b.rows[k * ROWW:(k + 1) * ROWW, :] + step
 
@@ -406,75 +426,91 @@
         hot = jnp.where(lax.broadcasted_iota(jnp.int32, (HOME, NG * EVICT), 0) == place, 1.0, 0.0).astype(BF16)
         b.home_out[...] = b.home[...] + mm(hot, b.ev_in[...].reshape(NG * EVICT, ROWW).astype(BF16))
 
-    def ag_copy(w, src, to):
-        lo, hi = ((0, FIRST), (FIRST, 7))[w]
+    def ag_copy(w, to):
+        lo, hi = SPANS[w]
         ss, rs = ((b.ag0_s, b.ag0_r), (b.ag1_s, b.ag1_r))[w]
         return pltpu.make_async_remote_copy(
-            b.final.at[lo:hi], b.out_all.at[lax.rem(src, 2), src // 8, lax.rem(src // 2, 4), lo:hi],
-            ss.at[0], rs.at[0], device_id=(to, p), device_id_type=MESH)
+            b.final.at[lo:hi], b.out_all.at[core, yl, x, lo:hi], ss.at[0], rs.at[0],
+            device_id=(to * 2 + core, p), device_id_type=MESH)
 
     def spread(w):
         def one(i, _):
-            ag_copy(w, g, lax.rem(g + i, NG)).start()
+            ag_copy(w, lax.rem(yl * 4 + x + i, 8)).start()
             return 0
 
-        lax.fori_loop(1, 16, one, 0)
-        lo, hi = ((0, FIRST), (FIRST, 7))[w]
+        lax.fori_loop(1, 8, one, 0)
+        lo, hi = SPANS[w]
         b.out_all[core, yl, x, lo:hi] = b.final[lo:hi]
+
+    pairs = []
+    for w, (lo, hi) in enumerate(SPANS):
+        pairs.append(pltpu.make_async_remote_copy(
+            b.out_all.at[core, :, :, lo:hi], b.out_all.at[core, :, :, lo:hi], b.fw_s.at[w], b.fw_r.at[w],
+            device_id=(g + 1 - 2 * core, p), device_id_type=MESH))
+
+    def forward(w):
+        lo, hi = SPANS[w]
+        await_bytes(b.ag_like.at[:, lo:hi], (b.ag0_r, b.ag1_r)[w].at[0])
+        pairs[w].start()
 
     def run_terms(lo, hi):
         lax.fori_loop(lo, hi, terms, 0)
 
+    loads["acc"].wait()
+    loads["bias"].wait()
+    loads["dest"].wait()
     rg[...] = jnp.zeros_like(rg)
+    merge(0)
+    xa[0][0]()
     run_terms(0, 1)
-    merge(0)
+    merge(1)
+    yb[0][0]()
+    run_terms(1, 2)
+    merge(2)
     zc[0]()
-    run_terms(1, 2)
-    merge(1)
-    xa[0][0]()
-    merge(2)
-    yb[0][0]()
+    run_terms(2, 3)
     merge(3)
+    xa[1][0]()
     merge(4)
-    run_terms(2, 6)
+    yb[1][0]()
+    run_terms(3, 6)
     xa[0][1]()
-    xa[1][0]()
+    run_terms(6, 7)
     yb[0][1]()
-    yb[1][0]()
-    run_terms(6, 10)
+    run_terms(7, 9)
+    xa[1][1]()
+    run_terms(9, 10)
+    yb[1][1]()
+    run_terms(10, 12)
     xa[0][2]()
     ya[0][0]()
-    xa[1][1]()
+    run_terms(12, 13)
     yb[0][2]()
     xb[0][0]()
-    yb[1][1]()
-    run_terms(10, 13)
     xa[1][2]()
     ya[1][0]()
     yb[1][2]()
     xb[1][0]()
-    ya[0][1]()
-    xb[0][1]()
     zc[1]()
     yc[0]()
     adagrad()
+    evict()
+    ya[0][1]()
+    xb[0][1]()
+    zw[0][0]()
     ya[1][1]()
     xb[1][1]()
-    ya[0][2]()
-    xb[0][2]()
-    zw[0][0]()
-    evict()
+    zw[1][0]()
     yc[1]()
     xc[0]()
-    ya[1][2]()
-    xb[1][2]()
-    zw[1][0]()
-    xc[1]()
     zw[0][1]()
     spread(0)
+    zw[1][1]()
+    xc[1]()
+    spread(1)
+    forward(0)
     settle_home()
-    zw[1][1]()
-    spread(1)
+    forward(1)
 
     for sems in ((b.hit_s, b.hit_r), (b.miss_s, b.miss_r)):
         for sem in sems:
@@ -485,9 +521,10 @@
         phase[-1]()
     own_hit.wait()
     own_miss.wait()
-    for (lo, hi), sems in (((0, FIRST), (b.ag0_s, b.ag0_r)), ((FIRST, 7), (b.ag1_s, b.ag1_r))):
-        for sem in sems:
-            await_bytes(b.ag_like.at[:, lo:hi], sem.at[0])
+    for (lo, hi), sem, pair in zip(SPANS, (b.ag0_s, b.ag1_s), pairs):
+        await_bytes(b.ag_like.at[:, lo:hi], sem.at[0])
+        pair.wait_send()
+        pair.wait_recv()
 
     def tile(c, t):
         part, tt = divmod(t, 7)
@@ -499,15 +536,21 @@
     for r in range(2):
         for c in range(27):
             b.gdown_out[8 * r:8 * r + 8, c * ROWW:(c + 1) * ROWW] = tile(1, 27 * r + c)
-    b.gbias_out[...] = tile(0, 54)
+    b.gbias_out[...] = tile(1, 54)
+
+
+PIECES = (4, 4, 2, 1, 1)
 
 
 def hand_on(n_in, w_in, h_in, u_in, d_in, b_in, n_out, w_out, h_out, u_out, d_out, b_out, sems):
     copies = []
     for k, (src, dst) in enumerate(zip((n_in, w_in, h_in, u_in, d_in), (n_out, w_out, h_out, u_out, d_out))):
-        c = pltpu.make_async_copy(src, dst, sems.at[k])
-        c.start()
-        copies.append(c)
+        pieces = PIECES[k]
+        size = src.shape[0] // pieces
+        for i in range(pieces):
+            rows = pl.ds(i * size, size)
+            pltpu.make_async_copy(src.at[rows], dst.at[rows], sems.at[k]).start()
+        copies.append(pltpu.make_async_copy(src, dst, sems.at[k]))
     b_out[0:ROWW] = b_in[0]
     b_out[ROWW:216] = b_in[1, 0:216 - ROWW]
     for c in copies:
@@ -528,7 +571,7 @@
     out = pl.pallas_call(
         kernel,
         out_shape=tuple(pltpu.VMEM(s.shape, F32) for s in shapes),
-        in_specs=[anyw, anyw, vmem, anyw, vmem, anyw, anyw, anyw, anyw, vmem, vmem] + [smem] * 6,
+        in_specs=[anyw] * 11 + [smem] * 6,
         out_specs=(vmem,) * 6,
         scratch_shapes=[s for _, s in scratch_list()],
         compiler_params=pltpu.CompilerParams(

time: 72.2 us -> 61.6 us (0.85)
  Pallas kernels: 71.4 us -> 60.7 us
    pallas_call x1, Pallas kernels: 69.2 us -> 58.5 us  [body(): pl.pallas_call(kernel, out_shape=tuple((pltpu.VMEM(s.shape, F32) for s in...]
where the time goes in v3:
time: 61.6 us; the launch traced here: 61.5 us
  Pallas kernels  60.7 us (99%)
  between operations  0.81 us (1%)
    pallas_call x1, Pallas kernels, body(): pl.pallas_call(kernel, out_shape=tuple((pltpu.VMEM(s.shape, F32) for s in...  58.5 us
    pallas_call x1, Pallas kernels, body(): pl.pallas_call(hand_on, out_shape=tuple(shapes[:5]) + (jax.ShapeDtypeStru...  2.23 us

profile of v3, /device:TPU:1, one launch (start us, length us, event | category | flops | bytes accessed | tf_op | source)
XLA Modules:
  0.0 61.5 jit_solution(9167909539916266231)
XLA Ops:
  0.6 58.5 %cross_step.1 = (f32[2048,128]{1,0:T(8,128)S(1)}, f32[2048,128]{1,0:T(8,128)S(1)}, f32[1024,128]{1,0:T(8,128)S(1)}, f32[216,256]{1,0:T(8,128)S(1)}, f32[16,3456]{1,0:T(8,128)S(1)}, /*index=5*/f32[8,128]{1,0:T(8,128)S(1)}) custom-call(bf16[384,128]{1,0:T(8,128)(2,1)} %refs_0_.1, bf16[384,3456]{1,0:T(8,128)(2,1)} %refs_1_.1, s32[26,384]{1,0:T(8,128)} %bitcast.3, ...), custom_call_target="tpu_custom_call" | custom-call | tf_op jit(solution)/shard_map/cross_step/pallas_call | solution.py:571
  59.1 2.2 %hand_on.1 = (f32[2048,128]{1,0:T(8,128)}, f32[2048,128]{1,0:T(8,128)}, f32[1024,128]{1,0:T(8,128)}, f32[216,256]{1,0:T(8,128)}, f32[16,3456]{1,0:T(8,128)}, /*index=5*/f32[216]{0:T(256)}) custom-call(f32[2048,128]{1,0:T(8,128)S(1)} %get-tuple-element.12.n_in, f32[2048,128]{1,0:T(8,128)S(1)} %get-tuple-element.13.w_in, ...), custom_call_target="tpu_custom_call" | custom-call | tf_op jit(solution)/shard_map/hand_on/pallas_call | solution.py:585

commit v4 on v3

--- a/solution.py
+++ b/solution.py
@@ -32,12 +32,19 @@
 
 def tile_place(peer, t):
     part, tt = divmod(t, 7)
-    return (peer // 8, peer % 8, part // 4, part % 4, tt)
+    yh, z, yl, x = peer // 8, peer % 8, part // 4, part % 4
+    for k, (lo, hi) in enumerate(PARTS):
+        if lo <= tt < hi:
+            place = ((x, yh, z, yl), (yh, yl, z, x), (z, yh, yl, x))[KINDS[k]]
+            return k, place + (tt - lo,)
 
 
 WAVES = (((0, 2), (2, 4)), ((5, 6), (6, 7)))
 Z_TILE = 4
 FIRST = 4
+PARTS = WAVES[0] + ((Z_TILE, Z_TILE + 1),) + WAVES[1]
+KINDS = (0, 1, 2, 0, 1)
+DIMS = ((4, 2, 8, 2), (2, 2, 8, 4), (8, 2, 2, 4))
 SPANS = ((0, FIRST), (FIRST, 7))
 LOOKS = ((0, 7), (7, 14), (14, 20), (20, 26))
 T = (8, 128)
@@ -57,12 +64,14 @@
         ("rg", v((LINE, FOLD * ROWW), F32)), ("delta", v((SLOTS, ROWW), F32)),
         ("hit_buf", v((NP, HIT, ROWW), F32)), ("miss_buf", v((NG, HIT, ROWW), F32)),
         ("ev_buf", v((NG, EVICT, ROWW), F32)), ("ev_in", v((NG, EVICT, ROWW), F32)),
-        ("grad", v((2, 2, 8, 2, 4, 7) + T, F32)), ("r0", v((2, 8, 2, 4, 7) + T, F32)),
         ("rc1", v((7, 2, 2, 4) + T, F32)), ("c1", v((2, 2, 4) + T, F32)), ("rc2", v((3, 4) + T, F32)),
         ("c2", v((4,) + T, F32)), ("rc3", v((3,) + T, F32)),
         ("final", v((7,) + T, F32)), ("out_all", v((2, 2, 4, 7) + T, F32)),
-        ("ag_like", v((7, 7) + T, F32)), ("fw_s", dma((2,))), ("fw_r", dma((2,))), ("in_sem", dma((11,))), ("out_sem", dma((2,))), ("core_s", dma((1,))), ("core_r", dma((5,))),
+        ("ag_like", v((7, 7) + T, F32)), ("fw_s", dma((2,))), ("fw_r", dma((2,))), ("in_sem", dma((11,))), ("out_sem", dma((2,))), ("core_s", dma((5,))), ("core_r", dma((5,))),
     ]
+    for k, (lo, hi) in enumerate(PARTS):
+        dims = DIMS[KINDS[k]] + (hi - lo,) + T
+        items += [("grad" + str(k), v((2,) + dims, F32)), ("r0" + str(k), v(dims, F32))]
     for name in ("hit", "miss", "ev", "ag0", "ag1"):
         items += [(name + "_s", dma((1,))), (name + "_r", dma((1,)))]
     for name in ("c1", "c2", "c3"):
@@ -71,8 +80,8 @@
         n = hi - lo
         k = str(w)
         items += [
-            ("ra1" + k, v((6, 8, 2, n) + T, F32)), ("a1" + k, v((2, 8, 2, n) + T, F32)),
-            ("rb1" + k, v((6, 4, 4, n) + T, F32)), ("b1" + k, v((8, 4, n) + T, F32)),
+            ("ra1" + k, v((6, 8, 2, n) + T, F32)), ("a1" + k, v((2, 2, 8, n) + T, F32)),
+            ("rb1" + k, v((6, 4, 4, n) + T, F32)), ("b1" + k, v((4, 8, n) + T, F32)),
             ("ra2" + k, v((3, 8, n) + T, F32)), ("rb2" + k, v((3, 8, n) + T, F32)),
             ("ab" + k, v((8, 2 * n) + T, F32)), ("rab" + k, v((7, 2 * n) + T, F32)),
         ]
@@ -205,12 +214,17 @@
     for lo, hi in LOOKS:
         look(lo, hi)
 
-    grad, r0 = b.grad, b.r0
-    parts = WAVES[0] + ((Z_TILE, Z_TILE + 1),) + WAVES[1]
+    grads_of = [getattr(b, "grad" + str(k)) for k in range(5)]
+    r0s = [getattr(b, "r0" + str(k)) for k in range(5)]
+
+    def store(array, peer, t, value):
+        k, place = tile_place(peer, t)
+        grads_of[k][(array,) + place] = value
+
     swaps = []
-    for k, (lo, hi) in enumerate(parts):
+    for k in range(5):
         swaps.append(pltpu.make_async_remote_copy(
-            grad.at[1 - core, :, :, :, :, lo:hi], r0.at[:, :, :, :, lo:hi], b.core_s.at[0], b.core_r.at[k],
+            grads_of[k].at[1 - core], r0s[k], b.core_s.at[k], b.core_r.at[k],
             device_id=(g + 1 - 2 * core, p), device_id_type=MESH))
 
     loads["up"].wait()
@@ -227,8 +241,7 @@
             d = mm(b.hidden_t[...], gated[:, c0 * ROWW:(c0 + n) * ROWW])
             for c in range(n):
                 for r in range(32):
-                    grad[(1,) + tile_place(r // 2, (r % 2) * 27 + c0 + c)] = (
-                        d[8 * r:8 * r + 8, c * ROWW:(c + 1) * ROWW])
+                    store(1, r // 2, (r % 2) * 27 + c0 + c, d[8 * r:8 * r + 8, c * ROWW:(c + 1) * ROWW])
             sums.append(d[RANK:RANK + 8, :])
         total = jnp.concatenate(sums + [jnp.zeros((8, 256), F32)], axis=1)
         first = lax.broadcasted_iota(jnp.int32, (8, ROWW), 0) == 0
@@ -237,8 +250,8 @@
             piece = total[:, start:start + 384]
             if 216 * q > start:
                 piece = pltpu.roll(piece, 384 - (216 * q - start), 1)
-            grad[(1,) + tile_place(q, 54)] = jnp.where(first, piece[:, 0:ROWW], piece[:, ROWW:2 * ROWW])
-            grad[(1,) + tile_place(q, 55)] = nil
+            store(1, q, 54, jnp.where(first, piece[:, 0:ROWW], piece[:, ROWW:2 * ROWW]))
+            store(1, q, 55, nil)
 
     def up_grad():
         b.back[...] = mm(gated[...], b.down[...], ((1,), (1,))).astype(BF16)
@@ -247,11 +260,10 @@
             for rr in range(16 * n):
                 r = c0 * 16 + rr
                 for c in range(2):
-                    grad[(0,) + tile_place(r // 27, (r % 27) * 2 + c)] = (
-                        u[8 * rr:8 * rr + 8, c * ROWW:(c + 1) * ROWW])
+                    store(0, r // 27, (r % 27) * 2 + c, u[8 * rr:8 * rr + 8, c * ROWW:(c + 1) * ROWW])
         for q in range(NP):
-            grad[(0,) + tile_place(q, 54)] = nil
-            grad[(0,) + tile_place(q, 55)] = nil
+            store(0, q, 54, nil)
+            store(0, q, 55, nil)
 
     @pl.when(core == 0)
     def _():
@@ -268,15 +280,16 @@
         down_grad()
 
     def merge(k):
-        lo, hi = parts[k]
         swaps[k].wait_recv()
+        mine, other = r0s[k], grads_of[k]
+        inner = mine.shape[1]
 
         def one(q, _):
-            i, j = q // 8, lax.rem(q, 8)
-            r0[i, j, :, :, lo:hi] = r0[i, j, :, :, lo:hi] + grad[core, i, j, :, :, lo:hi]
+            i, j = q // inner, lax.rem(q, inner)
+            mine[i, j] = mine[i, j] + other[core, i, j]
             return 0
 
-        lax.fori_loop(0, 16, one, 0)
+        lax.fori_loop(0, mine.shape[0] * inner, one, 0)
 
     def terms(i, _):
         cols = pl.ds(pl.multiple_of(ROWW + i * 256, ROWW), 256)
@@ -315,8 +328,12 @@
             copy(chunk(right, 0), 4, right), copy(chunk(left, 1), 5, left),
         ]
 
-        def start():
-            for c in copies[:4]:
+        def far_out():
+            for c in copies[:2]:
+                c.start()
+
+        def near_out():
+            for c in copies[2:4]:
                 c.start()
 
         def middle():
@@ -333,11 +350,11 @@
         def done():
             await_bytes(buf, ss.at[0])
 
-        return start, middle, finish, done
+        return far_out, near_out, middle, finish, done
 
     def direct(n, me, dev, chunk, buf, ss, rs, put):
         copies = []
-        for d in range(1, n):
+        for d in sorted(range(1, n), key=lambda d: -min(d, n - d)):
             to = lax.rem(me + d, n)
             copies.append(pltpu.make_async_remote_copy(
                 chunk(to), buf.at[d - 1], ss.at[0], rs.at[0], device_id=dev(to), device_id_type=MESH))
@@ -373,23 +390,31 @@
         t = {m: getattr(b, m + k) for m in (
             "ra1", "a1", "rb1", "b1", "ra2", "rb2", "ab", "rab", "xa", "yb", "ya", "xb", "z") if hasattr(b, m + k)}
         sems = {m: (getattr(b, m + k + "_s"), getattr(b, m + k + "_r")) for m in ("xa", "yb", "ya", "xb", "z")}
+
+        def put_a1(h, value, r=t["a1"]):
+            for c in range(2):
+                r[h, c] = value[:, c]
+
+        def put_b1(h, value, r=t["b1"]):
+            for c in range(4):
+                r[c, 4 * h:4 * h + 4] = value[:, c]
+
         xa.append(ring4(
-            x, at_x, lambda c, h, lo=alo, hi=ahi: r0.at[h, :, :, c, lo:hi], t["ra1"], *sems["xa"],
-            setter(t["a1"], lambda h: h)))
+            x, at_x, lambda c, h, r=r0s[3 * w]: r.at[c, h], t["ra1"], *sems["xa"], put_a1))
         yb.append(ring4(
-            y, at_y, lambda c, h, lo=blo, hi=bhi: r0.at[c // 2, 4 * h:4 * h + 4, lax.rem(c, 2), :, lo:hi],
-            t["rb1"], *sems["yb"], setter(t["b1"], lambda h: sl(4 * h, 4 * h + 4))))
+            y, at_y, lambda c, h, r=r0s[3 * w + 1]: r.at[c // 2, lax.rem(c, 2), 4 * h:4 * h + 4],
+            t["rb1"], *sems["yb"], put_b1))
         ya.append(direct(
-            4, y, at_y, lambda c, r=t["a1"]: r.at[c // 2, :, lax.rem(c, 2)], t["ra2"], *sems["ya"],
+            4, y, at_y, lambda c, r=t["a1"]: r.at[c // 2, lax.rem(c, 2)], t["ra2"], *sems["ya"],
             setter(t["ab"], lambda n=n: (slice(None), sl(0, n)))))
         xb.append(direct(
-            4, x, at_x, lambda c, r=t["b1"]: r.at[:, c], t["rb2"], *sems["xb"],
+            4, x, at_x, lambda c, r=t["b1"]: r.at[c], t["rb2"], *sems["xb"],
             setter(t["ab"], lambda n=n: (slice(None), sl(n, 2 * n)))))
         zw.append(direct(
             8, z, at_z, lambda c, r=t["ab"]: r.at[c], t["rab"], *sems["z"],
             setter(b.final, lambda lo=alo, hi=bhi: sl(lo, hi))))
     zc = direct(
-        8, z, at_z, lambda c: r0.at[:, c, :, :, Z_TILE], b.rc1, b.c1_s, b.c1_r, setter(b.c1, lambda: Ellipsis))
+        8, z, at_z, lambda c: r0s[2].at[c, :, :, :, 0], b.rc1, b.c1_s, b.c1_r, setter(b.c1, lambda: Ellipsis))
     yc = direct(
         4, y, at_y, lambda c: b.c1.at[c // 2, lax.rem(c, 2)], b.rc2, b.c2_s, b.c2_r, setter(b.c2, lambda: Ellipsis))
     xc = direct(4, x, at_x, lambda c: b.c2.at[c], b.rc3, b.c3_s, b.c3_r, setter(b.final, lambda: Z_TILE))
@@ -468,28 +493,31 @@
     run_terms(1, 2)
     merge(2)
     zc[0]()
-    run_terms(2, 3)
     merge(3)
     xa[1][0]()
+    xa[0][1]()
+    xa[1][1]()
     merge(4)
     yb[1][0]()
-    run_terms(3, 6)
-    xa[0][1]()
+    yb[0][1]()
+    yb[1][1]()
+    run_terms(2, 5)
+    xa[0][2]()
+    run_terms(5, 6)
+    yb[0][2]()
     run_terms(6, 7)
-    yb[0][1]()
-    run_terms(7, 9)
-    xa[1][1]()
-    run_terms(9, 10)
-    yb[1][1]()
-    run_terms(10, 12)
-    xa[0][2]()
+    xa[1][2]()
+    run_terms(7, 8)
+    yb[1][2]()
+    run_terms(8, 12)
+    xa[0][3]()
     ya[0][0]()
+    yb[0][3]()
+    xb[0][0]()
     run_terms(12, 13)
-    yb[0][2]()
-    xb[0][0]()
-    xa[1][2]()
+    xa[1][3]()
     ya[1][0]()
-    yb[1][2]()
+    yb[1][3]()
     xb[1][0]()
     zc[1]()
     yc[0]()
@@ -516,7 +544,8 @@
         for sem in sems:
             await_bytes(b.hit_buf.at[0:NP - 1], sem.at[0])
     await_bytes(b.ev_buf.at[0:NG - 1], b.ev_s.at[0])
-    await_bytes(r0, b.core_s.at[0])
+    for c in swaps:
+        c.wait_send()
     for phase in xa + yb + ya + xb + zw + [zc, yc, xc]:
         phase[-1]()
     own_hit.wait()

time: 61.6 us -> 61.2 us (level)
  no operation moved by 1% of the time
where the time goes in v4:
time: 61.2 us; the launch traced here: 61.1 us
  Pallas kernels  60.2 us (98%)
  between operations  0.81 us (1%)
    pallas_call x1, Pallas kernels, body(): pl.pallas_call(kernel, out_shape=tuple((pltpu.VMEM(s.shape, F32) for s in...  58 us
    pallas_call x1, Pallas kernels, body(): pl.pallas_call(hand_on, out_shape=tuple(shapes[:5]) + (jax.ShapeDtypeStru...  2.23 us

profile of v4, /device:TPU:1, one launch (start us, length us, event | category | flops | bytes accessed | tf_op | source)
XLA Modules:
  0.0 61.1 jit_solution(10809394925256296730)
XLA Ops:
  0.6 58.0 %cross_step.1 = (f32[2048,128]{1,0:T(8,128)S(1)}, f32[2048,128]{1,0:T(8,128)S(1)}, f32[1024,128]{1,0:T(8,128)S(1)}, f32[216,256]{1,0:T(8,128)S(1)}, f32[16,3456]{1,0:T(8,128)S(1)}, /*index=5*/f32[8,128]{1,0:T(8,128)S(1)}) custom-call(bf16[384,128]{1,0:T(8,128)(2,1)} %refs_0_.1, bf16[384,3456]{1,0:T(8,128)(2,1)} %refs_1_.1, s32[26,384]{1,0:T(8,128)} %bitcast.3, ...), custom_call_target="tpu_custom_call" | custom-call | tf_op jit(solution)/shard_map/cross_step/pallas_call | solution.py:600
  58.7 2.2 %hand_on.1 = (f32[2048,128]{1,0:T(8,128)}, f32[2048,128]{1,0:T(8,128)}, f32[1024,128]{1,0:T(8,128)}, f32[216,256]{1,0:T(8,128)}, f32[16,3456]{1,0:T(8,128)}, /*index=5*/f32[216]{0:T(256)}) custom-call(f32[2048,128]{1,0:T(8,128)S(1)} %get-tuple-element.12.n_in, f32[2048,128]{1,0:T(8,128)S(1)} %get-tuple-element.13.w_in, ...), custom_call_target="tpu_custom_call" | custom-call | tf_op jit(solution)/shard_map/hand_on/pallas_call | solution.py:614
